TPU v7x, 32 devices: a whole 2x2x4 slice. The times are simulated.
32 devices in a mesh: space: 8 (over z, y), fsdp: 4 (over x, core).
Axes of the slice: x: 2, y: 2, z: 4, core: 2. Of those that a mesh axis runs over, the one named last changes fastest.
Arguments:
- frames: float32 [2, 4, 2, 16, 16], P(None, 'fsdp', None, 'space'), may hold values from -5 to 5
- targets: float32 [2, 4, 2, 16, 16], P(None, 'fsdp', None, 'space'), may hold values from -5 to 5
- sizes: int32 [2, 4], P(None, 'fsdp'), may hold values from 8 to 16, as said below
- horizon: int32 [2, 4, 2, 16, 16], P(None, 'fsdp', None, 'space'), may hold values from 0 to 4
- conv_weight: float32 [12800, 1024], P('space', 'fsdp'), may hold values from -0.0546875 to 0.0546875
- conv_m: float32 [12800, 1024], P('space', 'fsdp'), may hold values from -4.7683716e-06 to 4.7683716e-06
- conv_v: float32 [12800, 1024], P('space', 'fsdp'), may hold values from 7.627756e-15 to 3.0511025e-14
- gates_vec: float32 [2, 1024], P(None, 'space'), may hold values from 0.5 to 1.5
- gates_m: float32 [2, 1024], P(None, 'space'), may hold values from -4.7683716e-06 to 4.7683716e-06
- gates_v: float32 [2, 1024], P(None, 'space'), may hold values from 7.627756e-15 to 3.0511025e-14
- chan_vec: float32 [3, 256], P(None, 'space'), may hold values from -4 to 4
- chan_m: float32 [3, 256], P(None, 'space'), may hold values from -4.7683716e-06 to 4.7683716e-06
- chan_v: float32 [3, 256], P(None, 'space'), may hold values from 7.627756e-15 to 3.0511025e-14
Outputs:
- loss: float32 [], replicated
- grad_norm: float32 [], replicated
- conv_new: float32 [12800, 1024], P('space', 'fsdp')
- conv_m_new: float32 [12800, 1024], P('space', 'fsdp')
- conv_v_new: float32 [12800, 1024], P('space', 'fsdp')
- gates_new: float32 [2, 1024], P(None, 'space')
- gates_m_new: float32 [2, 1024], P(None, 'space')
- gates_v_new: float32 [2, 1024], P(None, 'space')
- chan_new: float32 [3, 256], P(None, 'space')
- chan_m_new: float32 [3, 256], P(None, 'space')
- chan_v_new: float32 [3, 256], P(None, 'space')
- hidden_final: float32 [4, 16, 16, 256], P('fsdp', 'space')
- cell_final: float32 [4, 16, 16, 256], P('fsdp', 'space')
Inputs may be any that keep to these rules, and one draw needn't show every extreme that they name: `sizes`: each value is 8 or 16; stream 0 of every micro-batch has 16. `horizon`: the value 4 marks a pixel without a target.
All inputs are finite; a program needn't handle non-finite values.
Results may differ from a plain program's by a relative error of at most 0.00035.
The roundings to bfloat16 on the way count: a program that leaves them out, or rounds other values in their place, can miss the bound.
Values may be sent and summed in bfloat16 or wider, within the bound.
A program may use at most 256 MiB of HBM per device.

v0:
```python
import jax
import jax.numpy as jnp
from jax import lax
from jax.sharding import PartitionSpec as P

GROUPS = 32
HOR = 4
STEP = 10


EPS_NORM = 1e-05
CLIP = 0.01
RATE = 0.01
BETA1 = 0.9
BETA2 = 0.999
DECAY = 0.01
EPS_ADAM = 1e-08


def with_halo(shard, sides, width):
    for axis, dim in sides:
        count, length = (lax.axis_size(axis), shard.shape[dim])
        up = [(i, (i + 1) % count) for i in range(count - 1)]
        down = [(j, i) for i, j in up]
        last = lax.slice_in_dim(shard, length - width, length, axis=dim)
        first = lax.slice_in_dim(shard, 0, width, axis=dim)
        before = lax.ppermute(last, axis, up)
        after = lax.ppermute(first, axis, down)
        shard = jnp.concatenate([before, shard, after], axis=dim)
    return shard


def cell_head(gates, cell_prev, valid, head_w):
    width = cell_prev.shape[-1]
    gate_in = jax.nn.sigmoid(gates[..., :width])
    gate_forget = jax.nn.sigmoid(gates[..., width : 2 * width])
    gate_out = jax.nn.sigmoid(gates[..., 2 * width : 3 * width])
    candidate = jnp.tanh(gates[..., 3 * width :])
    cell_new = (gate_forget * cell_prev + gate_in * candidate) * valid
    hidden_new = gate_out * jnp.tanh(cell_new) * valid
    return (hidden_new, cell_new, jnp.sum(hidden_new * head_w, axis=-1))


def adam_update(weight, first, second, grad):
    first = BETA1 * first + (1.0 - BETA1) * grad
    second = BETA2 * second + (1.0 - BETA2) * grad * grad
    first_hat = first / (1.0 - BETA1**STEP)
    second_hat = second / (1.0 - BETA2**STEP)
    weight = weight - RATE * (first_hat / (jnp.sqrt(second_hat) + EPS_ADAM) + DECAY * weight)
    return (weight, first, second)


def gather_weights(conv_weight, gates_vec, chan_vec):
    col_block = lax.all_gather(conv_weight.astype(jnp.bfloat16), "fsdp", axis=1, tiled=True)
    kernel, gains, chans = (
        lax.all_gather(col_block, "space", axis=0, tiled=True),
        lax.all_gather(gates_vec.astype(jnp.bfloat16), "space", axis=1, tiled=True),
        lax.all_gather(chan_vec.astype(jnp.bfloat16), "space", axis=1, tiled=True),
    )
    inputs_n = kernel.shape[0] // 25
    gates_n = kernel.shape[1]
    flipped = (
        kernel.reshape(25, inputs_n, gates_n).transpose(0, 2, 1).reshape(25 * gates_n, inputs_n)
    )
    return (kernel, flipped, gains.astype(jnp.float32), chans.astype(jnp.float32))


def lifted_patches(joined):
    rows, cols = (joined.shape[1], joined.shape[2])
    padded = with_halo(joined, (("space", 1),), 2)
    padded = jnp.pad(padded, ((0, 0), (0, 0), (2, 2), (0, 0)))
    pieces = [padded[:, a : a + rows, b : b + cols, :] for a in range(5) for b in range(5)]
    return jnp.concatenate(pieces, -1).reshape(-1, 25 * joined.shape[3])


def spread_back(delta, flipped):
    rows, cols = (delta.shape[1], delta.shape[2])
    padded = with_halo(delta, (("space", 1),), 2)
    padded = jnp.pad(padded, ((0, 0), (0, 0), (2, 2), (0, 0)))
    pieces = [
        padded[:, 4 - a : 4 - a + rows, 4 - b : 4 - b + cols, :] for a in range(5) for b in range(5)
    ]
    stacked = jnp.concatenate(pieces, -1).reshape(-1, 25 * delta.shape[3])
    result = jnp.dot(stacked, flipped, preferred_element_type=jnp.float32)
    return result.reshape(delta.shape[0], rows, cols, -1)


def time_major(array):
    return jnp.moveaxis(array, 1, 0)


def forward(weights, seq, goal, chosen, inside, count, hweight):
    kernel, flipped, gains, chans = weights
    streams, nframes, rows, cols = seq.shape
    width = chans.shape[1]
    valid = inside[:, :, None, None]

    def forward_frame(carry, inputs):
        hidden, cell = carry
        pixels, target, picked = inputs
        lifted = (pixels[..., None] * chans[0] + chans[1]) * valid
        joined = jnp.concatenate([lifted, hidden], -1).astype(jnp.bfloat16)
        patches = lifted_patches(joined)
        pre = jnp.dot(patches, kernel, preferred_element_type=jnp.float32).reshape(
            streams, rows, cols, GROUPS, -1
        )
        weighted = pre * valid[..., None]
        first, second = lax.psum(
            (jnp.sum(weighted, axis=(1, 2, 4)), jnp.sum(weighted * pre, axis=(1, 2, 4))), "space"
        )
        centre = first / count[:, None]
        scale = lax.rsqrt(second / count[:, None] - centre * centre + EPS_NORM)
        normed = ((pre - centre[:, None, None, :, None]) * scale[:, None, None, :, None]).reshape(
            streams, rows, cols, 4 * width
        )
        gates = normed * gains[0] + gains[1]
        hidden_new, cell_new, output = cell_head(gates, cell, valid, chans[2])
        error = output - target
        sse = jnp.sum(picked * (error * error)[..., None], axis=(0, 1, 2))
        slope = 2.0 * error * jnp.sum(picked * hweight, axis=-1)
        return ((hidden_new, cell_new), (sse, (patches, normed, scale, cell, gates, slope)))

    zeros = jnp.zeros((streams, rows, cols, width), jnp.float32)
    (hidden, cell), (sse, kept) = lax.scan(
        forward_frame, (zeros, zeros), (time_major(seq), time_major(goal), time_major(chosen))
    )
    return (hidden, cell, jnp.sum(sse, axis=0), kept)


def backward(weights, kept, seq, inside, count):
    kernel, flipped, gains, chans = weights
    patches, normed, scale, cells, gates, slope = kept
    streams, nframes, rows, cols = seq.shape
    width = chans.shape[1]
    valid = inside[:, :, None, None]

    def cell_part(gate_vals, cell_prev, head_w):
        return cell_head(gate_vals, cell_prev, valid, head_w)

    def backward_frame(carry, inputs):
        d_hidden, d_cell, d_gain, d_bias, d_head, d_lift_w, d_lift_b = carry
        normed_t, scale_t, cell_prev, gates_t, slope_t, pixels = inputs
        unused, pull = jax.vjp(cell_part, gates_t, cell_prev, chans[2])
        d_gates, d_cell_prev, d_head_t = pull((d_hidden, d_cell, slope_t))
        d_normed = (d_gates * gains[0]).reshape(streams, rows, cols, GROUPS, -1)
        grouped = normed_t.reshape(streams, rows, cols, GROUPS, -1)
        masked = d_normed * valid[..., None]
        first, second = lax.psum(
            (jnp.sum(masked, axis=(1, 2, 4)), jnp.sum(masked * grouped, axis=(1, 2, 4))), "space"
        )
        first = (first / count[:, None])[:, None, None, :, None]
        second = (second / count[:, None])[:, None, None, :, None]
        d_pre = (
            scale_t[:, None, None, :, None]
            * (d_normed - first - grouped * second)
            * valid[..., None]
        )
        d_pre = d_pre.reshape(streams, rows, cols, -1).astype(jnp.bfloat16)
        d_joined = spread_back(d_pre, flipped)
        d_lifted = d_joined[..., :width] * valid
        carry_new = (
            d_joined[..., width:],
            d_cell_prev,
            d_gain + jnp.sum(d_gates * normed_t, axis=(0, 1, 2)),
            d_bias + jnp.sum(d_gates, axis=(0, 1, 2)),
            d_head + d_head_t,
            d_lift_w + jnp.sum(d_lifted * pixels[..., None], axis=(0, 1, 2)),
            d_lift_b + jnp.sum(d_lifted, axis=(0, 1, 2)),
        )
        return (carry_new, d_pre)

    zeros = jnp.zeros((streams, rows, cols, width), jnp.float32)
    wide_zero = jnp.zeros((4 * width,), jnp.float32)
    narrow_zero = jnp.zeros((width,), jnp.float32)
    start = (zeros, zeros, wide_zero, wide_zero, narrow_zero, narrow_zero, narrow_zero)
    final, d_pre_all = lax.scan(
        backward_frame, start, (normed, scale, cells, gates, slope, time_major(seq)), reverse=True
    )
    d_kernel = lax.dot_general(
        patches.reshape(-1, patches.shape[-1]),
        d_pre_all.reshape(-1, 4 * width),
        (((0,), (0,)), ((), ())),
        preferred_element_type=jnp.float32,
    )
    d_gains = jnp.stack([final[2], final[3]])
    d_chans = jnp.stack([final[5], final[6], final[4]])
    return (d_kernel, d_gains, d_chans)


def reduce_grads(d_kernel, d_gains, d_chans):
    col_part = lax.psum_scatter(d_kernel, "fsdp", scatter_dimension=1, tiled=True)
    kernel_part, gains_part, chans_part = (
        lax.psum_scatter(col_part, "space", scatter_dimension=0, tiled=True),
        lax.psum_scatter(d_gains, "space", scatter_dimension=1, tiled=True),
        lax.psum_scatter(d_chans, "space", scatter_dimension=1, tiled=True),
    )
    gains_part, chans_part = lax.psum((gains_part, chans_part), "fsdp")
    return (kernel_part, gains_part, chans_part)


def per_device(
    frames,
    targets,
    sizes,
    horizon,
    conv_weight,
    conv_m,
    conv_v,
    gates_vec,
    gates_m,
    gates_v,
    chan_vec,
    chan_m,
    chan_v,
):
    micro, streams, nframes, rows, cols = frames.shape
    width = chan_vec.shape[1] * lax.axis_size("space")
    total_rows = rows * lax.axis_size("space")
    row_ids = lax.axis_index("space") * rows + jnp.arange(rows, dtype=jnp.int32)
    inside = (row_ids[None, None, :] >= total_rows - sizes[:, :, None]).astype(jnp.float32)
    select = (horizon[..., None] == jnp.arange(HOR, dtype=jnp.int32)).astype(jnp.float32) * inside[
        :, :, None, :, None, None
    ]
    counts = lax.psum(jnp.sum(select, axis=(0, 1, 2, 3, 4)), ("space", "fsdp"))
    hweight = 1.0 / (HOR * jnp.maximum(counts, 1.0))
    group_count = sizes.astype(jnp.float32) * (cols * (4 * width // GROUPS))
    held = gather_weights(conv_weight, gates_vec, chan_vec)
    sse_total = jnp.zeros((HOR,), jnp.float32)
    summed = None
    for batch in range(micro):
        hidden, cell, sse, kept = forward(
            held,
            frames[batch],
            targets[batch],
            select[batch],
            inside[batch],
            group_count[batch],
            hweight,
        )
        sse_total = sse_total + sse
        grads = backward(held, kept, frames[batch], inside[batch], group_count[batch])
        summed = grads if summed is None else jax.tree.map(jnp.add, summed, grads)
    summed = reduce_grads(*summed)
    kernel_grad, gains_grad, chans_grad = summed
    leading = (lax.axis_index("fsdp") == 0).astype(jnp.float32)
    squares = jnp.sum(kernel_grad * kernel_grad) + leading * (
        jnp.sum(gains_grad * gains_grad) + jnp.sum(chans_grad * chans_grad)
    )
    sse_total, squares = lax.psum((sse_total, squares), ("space", "fsdp"))
    loss = jnp.sum(sse_total * hweight)
    norm = jnp.sqrt(squares)
    factor = jnp.minimum(1.0, CLIP / (norm + 1e-06))
    conv_new, conv_m_new, conv_v_new = adam_update(
        conv_weight, conv_m, conv_v, kernel_grad * factor
    )
    gates_new, gates_m_new, gates_v_new = adam_update(
        gates_vec, gates_m, gates_v, gains_grad * factor
    )
    chan_new, chan_m_new, chan_v_new = adam_update(chan_vec, chan_m, chan_v, chans_grad * factor)
    return (
        loss,
        norm,
        conv_new,
        conv_m_new,
        conv_v_new,
        gates_new,
        gates_m_new,
        gates_v_new,
        chan_new,
        chan_m_new,
        chan_v_new,
        hidden,
        cell,
    )


def solution(mesh):
    in_specs = (
        P(None, "fsdp", None, "space", None),
        P(None, "fsdp", None, "space", None),
        P(None, "fsdp"),
        P(None, "fsdp", None, "space", None),
        P("space", "fsdp"),
        P("space", "fsdp"),
        P("space", "fsdp"),
        P(None, "space"),
        P(None, "space"),
        P(None, "space"),
        P(None, "space"),
        P(None, "space"),
        P(None, "space"),
    )
    out_specs = (
        P(),
        P(),
        P("space", "fsdp"),
        P("space", "fsdp"),
        P("space", "fsdp"),
        P(None, "space"),
        P(None, "space"),
        P(None, "space"),
        P(None, "space"),
        P(None, "space"),
        P(None, "space"),
        P("fsdp", "space", None, None),
        P("fsdp", "space", None, None),
    )
    return jax.shard_map(
        per_device, mesh=mesh, in_specs=in_specs, out_specs=out_specs, check_vma=False
    )
```

profile of v0, /device:TPU:0, one launch (start us, length us, event | category | flops | bytes accessed | tf_op | source)
XLA Modules:
  0.0 1829.7 jit_solution(8676363601833765467)
XLA Ops:
  7.2 2.4 convert_element_type.120
  9.7 32.9 %all-gather.4.cloned.1.call-done = bf16[1600,1024]{1,0:T(8,128)(2,1)} async-done(((bf16[1600,256]{1,0:T(8,128)(2,1)}), bf16[1600,1024]{1,0:T(8,128)(2,1)}) %all-gather.4.cloned.1.call-update) | async-done | bytes 3276816 | tf_op jit(solution)/shard_map/all_gather | solution.py:54
  43.5 85.6 %psum.127 = f32[4]{0:T(128)S(1)} all-reduce(f32[4]{0:T(128)S(1)} %get-tuple-element.2344), channel_id=1, replica_groups=mesh['space'=8,'fsdp'=4] {'space','fsdp'}, use_global_device_ids=true, to_apply=%region_1.0 | all-reduce | flops 4 | bytes 32 | tf_op jit(solution)/shard_map/psum | solution.py:224
  129.4 26.9 %all_gather.15 = bf16[2,1024]{1,0:T(2,128)(2,1)S(1)} all-gather(bf16[2,128]{1,0:T(2,128)(2,1)S(1)} %convert_element_type.122), channel_id=1, replica_groups=mesh['space'=8,'fsdp'=4] {'space'}, dimensions={1}, use_global_device_ids=true | all-gather | bytes 4608 | tf_op jit(solution)/shard_map/all_gather | solution.py:57
  156.9 17.1 all-gather
  177.7 367.8 %all-gather.6.cloned.1.call-done = bf16[12800,1024]{1,0:T(8,128)(2,1)} async-done(((bf16[1600,1024]{1,0:T(8,128)(2,1)}), bf16[12800,1024]{1,0:T(8,128)(2,1)}) %all-gather.6.cloned.1.call-update) | async-done | bytes 26214416 | tf_op jit(solution)/shard_map/all_gather | solution.py:56
  545.5 35.7 %copy.72 = bf16[25,512,1024]{1,2,0:T(8,128)(2,1)} copy(bf16[25,512,1024]{2,1,0:T(8,128)(2,1)} %bitcast.770) | data formatting | bytes 52428800 | tf_op jit(solution)/shard_map/reshape | solution.py:63
  584.4 113.8 %while.116 = (s32[]{:T(128)}, bf16[1,2,16,256]{3,2,1,0:T(8,128)(2,1)S(1)}, f32[1,2,16,256]{3,2,1,0:T(8,128)S(1)}, f32[2,4]{1,0:T(2,128)}, bf16[2,32,12800]{2,1,0...) while((s32[]{:T(128)}, ...), condition=%wide.region_12.13_spmd.clone, body=%wide.region_2.12_spmd.clone.sunk | while | flops 840708992 | bytes 35979080 | solution.py:124
  587.2 2.3 collective-permute-start.1
  597.0 10.8 fusion.234
  608.2 21.8 %all-reduce.22 = (f32[1,32]{1,0:T(1,128)S(1)}, f32[1,32]{1,0:T(1,128)S(1)}) all-reduce(f32[1,32]{1,0:T(1,128)S(1)} %bitcast.932, f32[1,32]{1,0:T(1,128)S(1)} %bitcast.936), channel_id=1, replica_groups=mesh['space'=8,'fsdp'=4] {'space'}, use_global_device_ids=true, to_apply=%region_5.5 | all-reduce | flops 64 | bytes 512 | tf_op jit(solution)/shard_map/while/body/eval_jaxpr/psum | solution.py:108
  645.7 1.6 collective-permute-start.1
  654.3 10.8 fusion.234
  665.5 19.6 %all-reduce.22 = (f32[1,32]{1,0:T(1,128)S(1)}, f32[1,32]{1,0:T(1,128)S(1)}) all-reduce(f32[1,32]{1,0:T(1,128)S(1)} %bitcast.932, f32[1,32]{1,0:T(1,128)S(1)} %bitcast.936), channel_id=1, replica_groups=mesh['space'=8,'fsdp'=4] {'space'}, use_global_device_ids=true, to_apply=%region_5.5 | all-reduce | flops 64 | bytes 512 | tf_op jit(solution)/shard_map/while/body/eval_jaxpr/psum | solution.py:108
  698.2 101.1 %while.118 = (s32[]{:T(128)}, f32[1,2,16,256]{3,2,1,0:T(8,128)S(1)}, f32[1,2,16,256]{3,2,1,0:T(8,128)}, f32[1024]{0:T(1024)}, f32[1024]{0:T(1024)}, /*index=5*/f...) while((s32[]{:T(128)}, f32[1,2,16,256]{3,2,1,0:T(8,128)S(1)}, ...), condition=%wide.region_40.41_spmd.clone, body=%wide.region_28.40_spmd.clone.sunk | while | flops 841984832 | bytes 34602548 | solution.py:176
  706.3 17.1 all-reduce.24
  725.8 3.9 collective-permute-start.5
  731.6 4.2 collective-permute-done.4
  736.6 10.8 fusion.258
  756.9 18.0 all-reduce.24
  777.2 3.0 collective-permute-start.5
  782.2 4.2 collective-permute-done.4
  787.1 10.8 fusion.258
  799.3 20.1 %fusion.171 = f32[12800,1024]{1,0:T(8,128)} fusion(bf16[64,12800]{1,0:T(8,128)(2,1)S(1)} %bitcast.788, bf16[64,1024]{1,0:T(8,128)(2,1)S(1)} %bitcast.894), kind=kOutput, calls=%fused_computation.477 | convolution fusion | flops 1677721600 | bytes 54198272 | tf_op jit(solution)/shard_map/dot_general | solution.py:179
  822.7 111.8 %while.117 = (s32[]{:T(128)}, f32[1,2,16,256]{3,2,1,0:T(8,128)S(1)}, f32[1,2,16,256]{3,2,1,0:T(8,128)S(1)}, f32[2,4]{1,0:T(2,128)}, bf16[2,32,12800]{2,1,0:T(8,1...) while((s32[]{:T(128)}, f32[1,2,16,256]{3,2,1,0:T(8,128)S(1)}, ...), condition=%wide.region_24.25_spmd.clone, body=%wide.region_14.24_spmd.clone.sunk | while | flops 840700800 | bytes 36077384 | solution.py:124
  825.7 2.8 collective-permute-start.3
  835.5 10.8 fusion.244
  846.7 19.6 %all-reduce.23 = (f32[1,32]{1,0:T(1,128)S(1)}, f32[1,32]{1,0:T(1,128)S(1)}) all-reduce(f32[1,32]{1,0:T(1,128)S(1)} %bitcast.934, f32[1,32]{1,0:T(1,128)S(1)} %bitcast.938), channel_id=1, replica_groups=mesh['space'=8,'fsdp'=4] {'space'}, use_global_device_ids=true, to_apply=%region_17.17 | all-reduce | flops 64 | bytes 512 | tf_op jit(solution)/shard_map/while/body/eval_jaxpr/psum | solution.py:108
  890.5 10.8 fusion.244
  901.8 19.7 %all-reduce.23 = (f32[1,32]{1,0:T(1,128)S(1)}, f32[1,32]{1,0:T(1,128)S(1)}) all-reduce(f32[1,32]{1,0:T(1,128)S(1)} %bitcast.934, f32[1,32]{1,0:T(1,128)S(1)} %bitcast.938), channel_id=1, replica_groups=mesh['space'=8,'fsdp'=4] {'space'}, use_global_device_ids=true, to_apply=%region_17.17 | all-reduce | flops 64 | bytes 512 | tf_op jit(solution)/shard_map/while/body/eval_jaxpr/psum | solution.py:108
  935.1 101.0 %while.119 = (s32[]{:T(128)}, f32[1,2,16,256]{3,2,1,0:T(8,128)S(1)}, f32[1,2,16,256]{3,2,1,0:T(8,128)}, f32[1024]{0:T(1024)}, f32[1024]{0:T(1024)}, /*index=5*/f...) while((s32[]{:T(128)}, f32[1,2,16,256]{3,2,1,0:T(8,128)S(1)}, ...), condition=%wide.region_53.54_spmd.clone, body=%wide.region_41.53_spmd.clone.sunk | while | flops 841984832 | bytes 34602548 | solution.py:176
  943.1 17.1 all-reduce.25
  962.6 3.9 collective-permute-start.7
  968.5 4.2 collective-permute-done.6
  973.4 10.8 fusion.271
  993.6 18.0 all-reduce.25
  1014.0 3.0 collective-permute-start.7
  1019.1 4.1 collective-permute-done.6
  1023.9 10.8 fusion.271
  1036.1 33.5 %convolution_add_fusion = f32[12800,1024]{1,0:T(8,128)} fusion(f32[12800,1024]{1,0:T(8,128)} %fusion.171, bf16[64,12800]{1,0:T(8,128)(2,1)S(1)} %bitcast.789, bf16[64,1024]{1,0:T(8,128)(2,1)S(1)} %bitcast.893), kind=kOutput, calls=%fused_computation.430 | convolution fusion | flops 1690828800 | bytes 106627072 | tf_op jit(solution)/shard_map/dot_general | solution.py:179
  1072.4 352.1 %reduce-scatter.9.cloned.1.call-done = f32[12800,256]{1,0:T(8,128)} async-done(((f32[12800,1024]{1,0:T(8,128)}), f32[12800,256]{1,0:T(8,128)}) %reduce-scatter.9.cloned.1.call-update) | async-done | bytes 13107216 | tf_op jit(solution)/shard_map/reduce_scatter | solution.py:191
  1425.2 64.2 %reduce-scatter.15.cloned.1.call-done = f32[32,3]{1,0:T(8,128)} async-done(((f32[256,3]{1,0:T(8,128)}), f32[32,3]{1,0:T(8,128)}) %reduce-scatter.15.cloned.1.call-update) | async-done | bytes 400
  1490.2 64.3 %reduce-scatter.13.cloned.1.call-done = f32[128,2]{1,0:T(8,128)} async-done(((f32[1024,2]{1,0:T(8,128)}), f32[128,2]{1,0:T(8,128)}) %reduce-scatter.13.cloned.1.call-update) | async-done | bytes 1040
  1555.4 5.7 all-reduce.17
  1563.6 208.1 %reduce-scatter.11.cloned.1.call-done = f32[1600,256]{1,0:T(8,128)} async-done(((f32[12800,256]{1,0:T(8,128)}), f32[1600,256]{1,0:T(8,128)}) %reduce-scatter.11.cloned.1.call-update) | async-done | bytes 1638416 | tf_op jit(solution)/shard_map/reduce_scatter | solution.py:193
  1771.7 2.5 multiply_reduce_fusion.10
  1774.8 39.4 %all-reduce.16 = (f32[4]{0:T(128)S(1)}, f32[]{:T(128)}) all-reduce(f32[4]{0:T(128)S(1)} %add.570, f32[]{:T(128)S(6)} %add.575), channel_id=1, replica_groups=mesh['space'=8,'fsdp'=4] {'space','fsdp'}, use_global_device_ids=true, to_apply=%region_26.27 | all-reduce | flops 5 | bytes 40 | tf_op jit(solution)/shard_map/psum | solution.py:249
  1816.8 5.0 multiply_subtract_fusion
  (910 shorter events, 168.9 us)
Async XLA Ops:
  7.2 35.4 %all-gather.4.cloned.1.call-start = ((), (), s32[]{:S(2)}) async-start(), calls=%async_computation.4 | async-start | bytes 4096000 | tf_op jit(solution)/shard_map/all_gather | solution.py:54
  9.7 535.8 %all-gather.6.cloned.1.call-start = ((), (), s32[]{:S(2)}) async-start(), calls=%async_computation.5 | async-start | bytes 29491200 | tf_op jit(solution)/shard_map/all_gather | solution.py:56
  42.6 86.7 %copy-start.71 = (f32[2,128]{1,0:T(2,128)S(1)}, f32[2,128]{1,0:T(2,128)}, u32[]{:S(2)}) copy-start(f32[2,128]{1,0:T(2,128)} %param.28) | copy-start | bytes 3076
  42.6 114.3 %copy-start.64 = (f32[3,32]{1,0:T(4,128)S(1)}, f32[3,32]{1,0:T(4,128)}, u32[]{:S(2)}) copy-start(f32[3,32]{1,0:T(4,128)} %param.31) | copy-start | bytes 1156
  42.6 133.9 %copy-start.67 = (f32[2,1,2,2,16]{4,3,2,1,0:T(2,128)S(1)}, f32[2,1,2,2,16]{4,3,2,1,0:T(2,128)}, u32[]{:S(2)}) copy-start(f32[2,1,2,2,16]{4,3,2,1,0:T(2,128)} %param.22) | copy-start | bytes 1540
  42.6 133.9 %copy-start.68 = (f32[2,1,2,2,16]{4,3,2,1,0:T(2,128)S(1)}, f32[2,1,2,2,16]{4,3,2,1,0:T(2,128)}, u32[]{:S(2)}) copy-start(f32[2,1,2,2,16]{4,3,2,1,0:T(2,128)} %param.21) | copy-start | bytes 1540
  42.6 1381.8 %reduce-scatter.9.cloned.1.call-start = ((), (), s32[]{:S(2)}) async-start(), calls=%async_computation.6 | async-start | bytes 65536000 | tf_op jit(solution)/shard_map/reduce_scatter | solution.py:191
  129.1 452.1 %copy-start.78 = (f32[4]{0:T(128)}, f32[4]{0:T(128)S(1)}, u32[]{:S(2)}) copy-start(f32[4]{0:T(128)S(1)} %psum.127) | copy-start | bytes 52
  587.2 8.0 collective-permute-start.1
  589.5 6.3 collective-permute-start
  595.9 11.9 copy-start.4
  645.7 7.3 collective-permute-start.1
  647.3 5.8 collective-permute-start
  653.2 11.9 copy-start.4
  698.2 32.8 %copy-start.36 = (f32[1024]{0:T(1024)S(1)}, f32[1024]{0:T(1024)}, u32[]{:S(2)}) copy-start(f32[1024]{0:T(1024)} %get-tuple-element.3277) | copy-start | bytes 12292 | tf_op jit(solution)/shard_map/while
  698.2 32.8 %copy-start.39 = (f32[1024]{0:T(1024)S(1)}, f32[1024]{0:T(1024)}, u32[]{:S(2)}) copy-start(f32[1024]{0:T(1024)} %get-tuple-element.3276) | copy-start | bytes 12292 | tf_op jit(solution)/shard_map/while
  725.8 5.9 collective-permute-start.5
  729.7 6.2 collective-permute-start.4
  748.8 32.8 %copy-start.36 = (f32[1024]{0:T(1024)S(1)}, f32[1024]{0:T(1024)}, u32[]{:S(2)}) copy-start(f32[1024]{0:T(1024)} %get-tuple-element.3277) | copy-start | bytes 12292 | tf_op jit(solution)/shard_map/while
  748.8 32.8 %copy-start.39 = (f32[1024]{0:T(1024)S(1)}, f32[1024]{0:T(1024)}, u32[]{:S(2)}) copy-start(f32[1024]{0:T(1024)} %get-tuple-element.3276) | copy-start | bytes 12292 | tf_op jit(solution)/shard_map/while
  777.2 5.0 collective-permute-start.5
  780.2 6.2 collective-permute-start.4
  825.7 8.5 collective-permute-start.3
  828.5 5.8 collective-permute-start.2
  834.4 11.9 copy-start.5
  882.0 7.1 collective-permute-start.3
  883.5 5.9 collective-permute-start.2
  889.4 11.9 copy-start.5
  935.1 32.7 %copy-start.30 = (f32[1024]{0:T(1024)S(1)}, f32[1024]{0:T(1024)}, u32[]{:S(2)}) copy-start(f32[1024]{0:T(1024)} %get-tuple-element.3349) | copy-start | bytes 12292 | tf_op jit(solution)/shard_map/while
  935.1 32.7 %copy-start.33 = (f32[1024]{0:T(1024)S(1)}, f32[1024]{0:T(1024)}, u32[]{:S(2)}) copy-start(f32[1024]{0:T(1024)} %get-tuple-element.3348) | copy-start | bytes 12292 | tf_op jit(solution)/shard_map/while
  962.6 6.0 collective-permute-start.7
  966.5 6.2 collective-permute-start.6
  985.6 32.7 %copy-start.30 = (f32[1024]{0:T(1024)S(1)}, f32[1024]{0:T(1024)}, u32[]{:S(2)}) copy-start(f32[1024]{0:T(1024)} %get-tuple-element.3349) | copy-start | bytes 12292 | tf_op jit(solution)/shard_map/while
  985.6 32.7 %copy-start.33 = (f32[1024]{0:T(1024)S(1)}, f32[1024]{0:T(1024)}, u32[]{:S(2)}) copy-start(f32[1024]{0:T(1024)} %get-tuple-element.3348) | copy-start | bytes 12292 | tf_op jit(solution)/shard_map/while
  1014.0 5.1 collective-permute-start.7
  1017.0 6.2 collective-permute-start.6
  1069.7 419.7 %reduce-scatter.15.cloned.1.call-start = ((), (), s32[]{:S(2)}) async-start(), calls=%async_computation.9 | async-start | bytes 147456
  1071.1 483.4 %reduce-scatter.13.cloned.1.call-start = ((), (), s32[]{:S(2)}) async-start(), calls=%async_computation.8 | async-start | bytes 589824
  1072.3 699.3 %reduce-scatter.11.cloned.1.call-start = ((), (), s32[]{:S(2)}) async-start(), calls=%async_computation.7 | async-start | bytes 14745600 | tf_op jit(solution)/shard_map/reduce_scatter | solution.py:193
  1424.4 392.3 %copy-start.13 = (f32[1600,256]{1,0:T(8,128)S(1)}, f32[1600,256]{1,0:T(8,128)}, u32[]{:S(2)}) copy-start(f32[1600,256]{1,0:T(8,128)} %param.26) | copy-start | bytes 4915204
  1424.5 390.4 %copy-start.79 = (f32[4]{0:T(128)S(1)}, f32[4]{0:T(128)}, u32[]{:S(2)}) copy-start(f32[4]{0:T(128)} %copy-done.78) | copy-start | bytes 52
  1424.5 391.0 %copy-start.72 = (f32[2,128]{1,0:T(2,128)S(1)}, f32[2,128]{1,0:T(2,128)}, u32[]{:S(2)}) copy-start(f32[2,128]{1,0:T(2,128)} %param.28) | copy-start | bytes 3076
  1424.5 391.0 %copy-start.73 = (f32[2,128]{1,0:T(2,128)S(1)}, f32[2,128]{1,0:T(2,128)}, u32[]{:S(2)}) copy-start(f32[2,128]{1,0:T(2,128)} %param.29) | copy-start | bytes 3076
  1424.5 391.0 %copy-start.74 = (f32[2,128]{1,0:T(2,128)S(1)}, f32[2,128]{1,0:T(2,128)}, u32[]{:S(2)}) copy-start(f32[2,128]{1,0:T(2,128)} %param.30) | copy-start | bytes 3076
  1424.5 391.6 %copy-start.65 = (f32[3,32]{1,0:T(4,128)S(1)}, f32[3,32]{1,0:T(4,128)}, u32[]{:S(2)}) copy-start(f32[3,32]{1,0:T(4,128)} %param.31) | copy-start | bytes 1156
  1424.5 391.6 %copy-start.69 = (f32[3,32]{1,0:T(4,128)S(1)}, f32[3,32]{1,0:T(4,128)}, u32[]{:S(2)}) copy-start(f32[3,32]{1,0:T(4,128)} %param.32) | copy-start | bytes 1156
  1424.5 391.6 %copy-start.70 = (f32[3,32]{1,0:T(4,128)S(1)}, f32[3,32]{1,0:T(4,128)}, u32[]{:S(2)}) copy-start(f32[3,32]{1,0:T(4,128)} %param.33) | copy-start | bytes 1156
  1424.6 392.2 %copy-start.6 = (f32[1600,256]{1,0:T(8,128)S(1)}, f32[1600,256]{1,0:T(8,128)}, u32[]{:S(2)}) copy-start(f32[1600,256]{1,0:T(8,128)} %param.25) | copy-start | bytes 4915204
  (102 other events, 531.6 us)
Sparse Core Ops, SparseCore 0:
  10.1 32.3 all-gather.3
  44.1 501.3 all-gather.5
  1069.8 354.5 reduce-scatter.8
  1428.5 60.8 reduce-scatter.14
  1493.5 60.9 reduce-scatter.12
  1558.0 213.5 reduce-scatter.10
where the time goes:
time: 1840 us; the launch traced here: 1830 us
  waiting for transfers between devices  1110 us (60%)
  blocking collectives  326 us (18%)
  matrix products  140 us (8%)
  local copies, waits for them, and re-layouts  122 us (7%)
  other arithmetic  79.4 us (4%)
  starting transfers between devices  32.7 us (2%)
    all_gather x1, waiting for transfers between devices, gather_weights(): lax.all_gather(col_block, 'space', axis=0, tiled=True)  368 us
    reduce_scatter x1, waiting for transfers between devices, reduce_grads(): lax.psum_scatter(d_kernel, 'fsdp', scatter_dimension=1, tiled=True)  352 us
    reduce_scatter x1, waiting for transfers between devices, reduce_grads(): lax.psum_scatter(col_part, 'space', scatter_dimension=0, tiled=True)  208 us
    unnamed x8, waiting for transfers between devices  129 us
    psum x1, blocking collectives, per_device(): counts = lax.psum(jnp.sum(select, axis=(0, 1, 2, 3, 4)), ('space', 'fsdp'))  85.6 us
    psum x4, blocking collectives, forward_frame(): lax.psum((jnp.sum(weighted, axis=(1, 2, 4)), jnp.sum(weighted * pre, axis...  80.7 us
    psum x4, blocking collectives, backward_frame(): lax.psum((jnp.sum(masked, axis=(1, 2, 4)), jnp.sum(masked * grouped, axis...  70.3 us
    dot_general x2, matrix products, backward(): lax.dot_general(patches.reshape(-1, patches.shape[-1]), d_pre_all.reshape...  53.6 us
  transfers between devices with their start and end apart: 22, of which 14 were waited for; matrix products, arithmetic and copies ran while one was open for 2% of the time, Pallas kernels for 0%

commit v1 on v0

--- a/solution.py
+++ b/solution.py
@@ -1,6 +1,10 @@
+import functools
+
 import jax
 import jax.numpy as jnp
 from jax import lax
+from jax.experimental import pallas as pl
+from jax.experimental.pallas import tpu as pltpu
 from jax.sharding import PartitionSpec as P
 
 GROUPS = 32
@@ -274,6 +278,962 @@
     )
 
 
+MESH = pl.DeviceIdType.MESH
+F32 = jnp.float32
+BF16 = jnp.bfloat16
+TAPS = 25
+
+
+def low(v):
+    return v.astype(BF16).astype(F32)
+
+
+def dot(a, b):
+    return jnp.dot(a, b, preferred_element_type=F32)
+
+
+def dot_nt(a, b):
+    return lax.dot_general(a, b, (((1,), (1,)), ((), ())), preferred_element_type=F32)
+
+
+def step_kernel(
+    geo,
+    frames_in,
+    targets_in,
+    horizon_in,
+    sizes_in,
+    gates_in,
+    chan_in,
+    w_ref,
+    m_ref,
+    v_ref,
+    grad,
+    wf,
+    m_out,
+    v_out,
+    small_ref,
+    h_ref,
+    c_ref,
+    frames_ref,
+    targets_ref,
+    horizon_ref,
+    sizes_ref,
+    gates_ref,
+    chan_ref,
+    stage,
+    wr,
+    wl,
+    wh,
+    wht,
+    tiles,
+    pix,
+    cols,
+    xb,
+    sa,
+    sb,
+    pre1,
+    save,
+    h1,
+    yrow,
+    dst,
+    dhp,
+    dhy,
+    dhr,
+    d_own,
+    dall,
+    dt,
+    ht,
+    hr,
+    xt,
+    ps,
+    vt,
+    vf,
+    vs,
+    qf,
+    qs,
+    in_sem,
+    w_sem,
+    local_sem,
+    sp_send,
+    sp_recv,
+    wsend,
+    wrecv,
+    wfs,
+    wfr,
+    f_send,
+    f_recv,
+):
+    S, F, R, rows, PX = geo
+    width = 8 * 32
+    s, f = lax.axis_index("space"), lax.axis_index("fsdp")
+    xx, cc = f // 2, lax.rem(f, 2)
+    f_x, f_c, f_d = (1 - xx) * 2 + cc, xx * 2 + 1 - cc, (1 - xx) * 2 + 1 - cc
+    fpeers = (f_x, f_c, f_d)
+    pending = []
+
+    def ahead(k):
+        return lax.rem(s + k, S)
+
+    def behind(k):
+        return lax.rem(s - k + S, S)
+
+    def only(when, do):
+        if when is None:
+            do()
+        else:
+            pl.when(when)(do)
+
+    def copy_to(src, dst_, ssem, rsem, dev, when=None):
+        cp = pltpu.make_async_remote_copy(
+            src_ref=src, dst_ref=dst_, send_sem=ssem, recv_sem=rsem,
+            device_id=dev, device_id_type=MESH,
+        )
+        pending.append((cp, when))
+        return cp
+
+    def send(src, dst_, ssem, rsem, dev, when=None):
+        cp = copy_to(src, dst_, ssem, rsem, dev, when)
+        only(when, cp.start)
+
+    def landing(slot, rsem):
+        return pltpu.make_async_remote_copy(
+            src_ref=slot, dst_ref=slot, send_sem=rsem, recv_sem=rsem,
+            device_id=(s, f_c), device_id_type=MESH,
+        )
+
+    def arrived(slot, rsem, when=None):
+        only(when, landing(slot, rsem).wait_recv)
+
+    barrier = pltpu.get_barrier_semaphore()
+    for k in range(1, S):
+        pl.semaphore_signal(barrier, inc=1, device_id=(ahead(k), f), device_id_type=MESH)
+    for p in fpeers:
+        pl.semaphore_signal(barrier, inc=1, device_id=(s, p), device_id_type=MESH)
+    small_ins = []
+    for n, (src, held) in enumerate(
+        (
+            (frames_in, frames_ref), (targets_in, targets_ref), (horizon_in, horizon_ref),
+            (sizes_in, sizes_ref), (gates_in, gates_ref), (chan_in, chan_ref),
+        )
+    ):
+        small_ins.append(pltpu.make_async_copy(src, held, in_sem.at[n]))
+        small_ins[-1].start()
+    base = lax.rem(s * R, 2 * width)
+    zero_rows = jnp.zeros((2 * width, wf.shape[1]), F32)
+    wf[0 : 2 * width, :] = zero_rows
+    wf[wf.shape[0] - 2 * width :, :] = zero_rows
+    get_w = []
+    for q in range(4):
+        own_w = wf.at[pl.ds(pl.multiple_of(base + R // 4 * q, 16), R // 4), :]
+        get_w.append(
+            pltpu.make_async_copy(w_ref.at[R // 4 * q : R // 4 * (q + 1), :], own_w, w_sem.at[q])
+        )
+        get_w[-1].start()
+
+    for cp in small_ins:
+        cp.wait()
+
+    def line(ref):
+        parts = [
+            ref[m, 0, t, r : r + 1, :].astype(F32)
+            for t in range(2) for r in range(2) for m in range(2)
+        ]
+        return jnp.concatenate(parts, axis=1)
+
+    lane128 = lax.broadcasted_iota(jnp.int32, (1, 128), 1)
+    tall = jnp.where(lax.rem(lane128 // 16, 2) == 0, sizes_ref[0:1, 0:1], sizes_ref[0:1, 1:2])
+    chans = [chan_ref[q : q + 1, :] for q in range(3)] + [jnp.zeros((1, 32), F32)]
+    tiles[f, s] = jnp.concatenate(
+        [
+            line(frames_ref), line(targets_ref), line(horizon_ref), gates_ref[...],
+            jnp.concatenate(chans, axis=1), tall.astype(F32), jnp.zeros((1, 128), F32),
+        ],
+        axis=0,
+    )
+    pl.semaphore_wait(barrier, S - 1 + 3)
+
+    for k in range(1, S):
+        send(tiles.at[f, s], tiles.at[f, s], sp_send.at[0, k], sp_recv.at[0, k], (ahead(k), f))
+
+    def holds(src, kind, i):
+        lo = 512 * i + 256 * kind
+        if all((q * R) % 512 + R > lo and (q * R) % 512 < lo + 256 for q in range(S)):
+            return None
+        first = lax.rem(src * R, 512)
+        return (lo < first + R) & (lo + 256 > first)
+
+    def stage_slot(kind, i):
+        for j in range(2):
+            r0 = 512 * i + 256 * kind + 128 * j
+            block = wf[r0 : r0 + 128, :].T.astype(BF16)
+            stage[kind, i, j] = block.reshape(8, 32, 128)
+
+    def send_slot(kind, i):
+        when = holds(s, kind, i)
+        for k in range(1, S):
+            to = ahead(k)
+            send(
+                stage.at[kind, i, :, to], wr.at[s, kind, i, :, f],
+                wsend.at[kind, i, k], wrecv.at[kind, i, k], (to, f), when,
+            )
+
+    for i, q in ((0, (0,)), (1, (1,)), (2, (2, 3)), (3, ())):
+        for n in q:
+            get_w[n].wait()
+        stage_slot(0, i)
+        send_slot(0, i)
+    stage_slot(1, 0)
+    stage_slot(1, 1)
+    for i in range(4):
+        wr[s, 0, i, :, f] = stage[0, i, :, s]
+
+    for k in range(1, S):
+        arrived(tiles.at[f, behind(k)], sp_recv.at[0, k])
+    for n, p in enumerate(fpeers):
+        send(tiles.at[f], tiles.at[f], f_send.at[0, n], f_recv.at[0, n], (s, p))
+
+    lane = lax.broadcasted_iota(jnp.int32, (1, PX), 1)
+    row_of = lane // 32
+    micro_of = lax.rem(lane // 16, 2)
+    col_of = lax.rem(lane, 16)
+
+    def build_pix(p):
+        for t in range(2):
+            halves = []
+            for k in range(4):
+                left = tiles[p, 2 * k][:, t * 64 : t * 64 + 64]
+                right = tiles[p, 2 * k + 1][:, t * 64 : t * 64 + 64]
+                halves.append(jnp.concatenate([left, right], axis=1))
+            whole = jnp.concatenate(halves, axis=1)
+            within = (row_of.astype(F32) >= rows - whole[6:7, :]).astype(F32)
+            sub = lax.broadcasted_iota(jnp.int32, (8, PX), 0)
+            pix[p, t] = jnp.where(sub == 7, within, whole)
+
+    build_pix(f)
+
+    sub32 = lax.broadcasted_iota(jnp.int32, (32, 128), 0)
+    lane32 = lax.broadcasted_iota(jnp.int32, (32, 128), 1)
+
+    def column(row, first):
+        picked = jnp.where(lane32 == sub32 + first, row, 0.0)
+        return low(jnp.sum(picked, axis=1, keepdims=True))
+
+    for g in range(4):
+        at = 2 * g + s // 4
+        off = 32 * lax.rem(s, 4)
+        for q in range(2):
+            cols[q, 32 * g : 32 * g + 32, :] = jnp.broadcast_to(
+                column(tiles[f, at][3 + q : 4 + q, :], off), (32, 128)
+            )
+    cols[2, 0:32, :] = jnp.broadcast_to(column(tiles[f, s][5:6, :], 64), (32, 128))
+    for k in range(8):
+        row5 = tiles[f, k][5:6, :]
+        for q in range(2):
+            cols[3 + q, 32 * k : 32 * k + 32, :] = jnp.broadcast_to(
+                column(row5, 32 * q), (32, 128)
+            )
+
+    gain, shift, head = cols[0, 0:128, 0:1], cols[1, 0:128, 0:1], cols[2, 0:32, 0:1]
+
+    def lifted(pixels, within):
+        return ((pixels * cols[3, :, 0:1] + cols[4, :, 0:1]) * within).astype(BF16)
+
+    inside = pix[f, 0, 7:8, :]
+
+    def relay(kind):
+        def first_hop(i, k):
+            src = behind(k)
+            when = holds(src, kind, i)
+            block = wr.at[src, kind, i, :, f]
+            to_x = copy_to(block, block, wfs.at[kind, i, k, 0], wfr.at[kind, i, k, 0], (s, f_x), when)
+            to_c = copy_to(block, block, wfs.at[kind, i, k, 1], wfr.at[kind, i, k, 1], (s, f_c), when)
+            here = landing(block, wrecv.at[kind, i, k]) if k > 0 else None
+
+            def hop():
+                if k > 0:
+                    here.wait_recv()
+                to_x.start()
+                to_c.start()
+
+            only(when, hop)
+
+        def second_hop(i, k):
+            src = behind(k)
+            when = holds(src, kind, i)
+            block = wr.at[src, kind, i, :, f_x]
+            to_c = copy_to(block, block, wfs.at[kind, i, k, 2], wfr.at[kind, i, k, 2], (s, f_c), when)
+            here = landing(block, wfr.at[kind, i, k, 0])
+
+            def hop():
+                here.wait_recv()
+                to_c.start()
+
+            only(when, hop)
+
+        for i in range(4):
+            for k in range(S):
+                first_hop(i, k)
+            if kind == 0 and i > 0:
+                send_slot(1, i - 1)
+            if kind == 0 and i == 3:
+                send_slot(1, 3)
+            if i > 0:
+                for k in range(S):
+                    second_hop(i - 1, k)
+        for k in range(S):
+            second_hop(3, k)
+        for i in range(4):
+            for k in range(S):
+                src = behind(k)
+                when = holds(src, kind, i)
+                own_c = landing(wr.at[src, kind, i, :, f_c], wfr.at[kind, i, k, 1])
+                far_c = landing(wr.at[src, kind, i, :, f_d], wfr.at[kind, i, k, 2])
+
+                def both():
+                    own_c.wait_recv()
+                    far_c.wait_recv()
+
+                only(when, both)
+
+    def merge(kind, out):
+        for tap in range(TAPS):
+            lo = 512 * tap + 256 * kind
+            total = None
+            for sp in range(S):
+                if sp * R < lo + 256 and sp * R + R > lo:
+                    part = wr[sp, kind, tap - (sp * R) // 512]
+                    total = part if total is None else total + part
+            total = total.reshape(2, 128, 128)
+            a, b = tap // 5, tap % 5
+            out[128 * a : 128 * a + 128, 256 * b : 256 * b + 128] = total[0]
+            out[128 * a : 128 * a + 128, 256 * b + 128 : 256 * b + 256] = total[1]
+
+    cmask = [
+        ((col_of + (b - 2) >= 0) & (col_of + (b - 2) < 16)).astype(F32) for b in range(5)
+    ]
+    rmask = [
+        ((row_of + (a - 2) >= 0) & (row_of + (a - 2) < rows)).astype(F32) for a in range(5)
+    ]
+
+    def slide(v, d):
+        if d == 0:
+            return v
+        parts = [
+            pltpu.roll(v[:, q : q + 128], (-d) % 128, 1) for q in range(0, v.shape[1], 128)
+        ]
+        return jnp.concatenate(parts, axis=1) * cmask[d + 2]
+
+    def conv(weights):
+        sa[...] = dot(weights[...], xb[...]).reshape(5, 128, PX)
+        out = sa[2]
+        for a in (0, 1, 3, 4):
+            out = out + pltpu.roll(sa[a], (-32 * (a - 2)) % PX, 1) * rmask[a]
+        return out
+
+    def slid_lift(t):
+        line = jnp.concatenate([pix[f, t, 0:1, :], inside], axis=0)
+        for b in range(5):
+            moved = slide(line, b - 2)
+            xb[256 * b : 256 * b + 256, :] = lifted(moved[0:1], moved[1:2])
+
+    count = pix[f, 0, 6:7, :] * (16.0 * 32.0)
+
+    def per_stream(v):
+        first = jnp.sum(jnp.where(micro_of == 0, v, 0.0), axis=1, keepdims=True)
+        second = jnp.sum(jnp.where(micro_of == 0, 0.0, v), axis=1, keepdims=True)
+        return jnp.where(micro_of == 0, first, second)
+
+    def cell_forward(t, pre, cell_prev):
+        groups = [pre[32 * g : 32 * g + 32, :] for g in range(4)]
+        sums = [
+            jnp.sum(v * inside, axis=0, keepdims=True) for v in groups
+        ] + [jnp.sum(v * inside * v, axis=0, keepdims=True) for v in groups]
+        sums = per_stream(jnp.concatenate(sums, axis=0)) / count
+        centre = sums[0:4]
+        scale = lax.rsqrt(sums[4:8] - centre * centre + EPS_NORM)
+        acts = []
+        for g in range(4):
+            normed = (groups[g] - centre[g : g + 1]) * scale[g : g + 1]
+            save[t, 0, 32 * g : 32 * g + 32, :] = normed
+            z = normed * gain[32 * g : 32 * g + 32] + shift[32 * g : 32 * g + 32]
+            act = jnp.tanh(z) if g == 3 else 1.0 / (1.0 + jnp.exp(-z))
+            save[t, 1, 32 * g : 32 * g + 32, :] = act
+            acts.append(act)
+        i, fo, o, cand = acts
+        cell = i * cand * inside if cell_prev is None else (fo * cell_prev + i * cand) * inside
+        tanh_c = jnp.tanh(cell)
+        hidden = o * tanh_c * inside
+        save[t, 2, 0:8, :] = jnp.concatenate([scale, scale], axis=0)
+        save[t, 2, 32:64, :] = cell
+        save[t, 2, 64:96, :] = tanh_c
+        save[t, 2, 96:128, :] = hidden
+        yrow[s, t : t + 1, :] = jnp.sum(hidden * head, axis=0, keepdims=True)
+        return hidden, cell
+
+    moments = [
+        pltpu.make_async_copy(m_ref, m_out, in_sem.at[6]),
+        pltpu.make_async_copy(v_ref, v_out, in_sem.at[7]),
+    ]
+    for cp in moments:
+        cp.start()
+    stage_slot(1, 2)
+    stage_slot(1, 3)
+    for i in range(4):
+        wr[s, 1, i, :, f] = stage[1, i, :, s]
+    slid_lift(0)
+    relay(0)
+    merge(0, wl)
+    hidden0, cell0 = cell_forward(0, conv(wl), None)
+    mine = pl.ds(pl.multiple_of(32 * s, 32), 32)
+    h1[f, mine, :] = hidden0.astype(BF16)
+    for k in range(1, S):
+        send(h1.at[f, mine, :], h1.at[f, mine, :], sp_send.at[1, k], sp_recv.at[1, k], (ahead(k), f))
+
+    relay(1)
+    slid_lift(1)
+    pre1[...] = conv(wl)
+    merge(1, wh)
+    for a in range(5):
+        for b in range(5):
+            block = wh[128 * a : 128 * a + 128, 256 * b : 256 * b + 256]
+            wht[256 * a : 256 * a + 256, 128 * b : 128 * b + 128] = block.astype(F32).T.astype(BF16)
+    for k in range(1, S):
+        their = pl.ds(pl.multiple_of(32 * behind(k), 32), 32)
+        arrived(h1.at[f, their, :], sp_recv.at[1, k])
+    send(h1.at[f], h1.at[f], f_send.at[1, 0], f_recv.at[1, 0], (s, f_x))
+    send(h1.at[f], h1.at[f], f_send.at[1, 1], f_recv.at[1, 1], (s, f_c))
+    hidden_in = h1[f].astype(F32)
+    for b in range(5):
+        xb[256 * b : 256 * b + 256, :] = slide(hidden_in, b - 2).astype(BF16)
+    pre1[...] = pre1[...] + conv(wh)
+    hidden1, cell1 = cell_forward(1, pre1[...], cell0)
+    for k in range(1, S):
+        send(yrow.at[s], yrow.at[s], sp_send.at[2, k], sp_recv.at[2, k], (ahead(k), f))
+
+    for n, p in enumerate(fpeers):
+        arrived(tiles.at[p], f_recv.at[0, n])
+    for p in fpeers:
+        build_pix(p)
+    weight_rows = []
+    for k in range(HOR):
+        total = None
+        for p in range(F):
+            for t in range(2):
+                picked = jnp.where(pix[p, t, 2:3, :] == float(k), pix[p, t, 7:8, :], 0.0)
+                total = picked if total is None else total + picked
+        counted = jnp.sum(total, axis=1, keepdims=True)
+        weight_rows.append(1.0 / (HOR * jnp.maximum(counted, 1.0)))
+    state = jnp.concatenate([hidden1, cell1, hidden1, cell1], axis=0).T
+    state = state.reshape(rows // 2, 2, 2, 16, 128)
+    ht[...] = jnp.where(
+        lax.broadcasted_iota(jnp.int32, (rows // 2, 16, 128), 2) < 64,
+        state[:, 0, 1], state[:, 1, 1],
+    )
+    for k in range(1, S):
+        send(ht.at[ahead(k)], hr.at[s], sp_send.at[6, k], sp_recv.at[6, k], (ahead(k), f))
+    hr[s] = ht[s]
+
+    for k in range(1, S):
+        arrived(yrow.at[behind(k)], sp_recv.at[2, k])
+    ysum = yrow[0]
+    for k in range(1, S):
+        ysum = ysum + yrow[k]
+    slopes, sse = [], [None] * HOR
+    for t in range(2):
+        err = ysum[t : t + 1] - pix[f, t, 1:2, :]
+        which = pix[f, t, 2:3, :]
+        hw = jnp.zeros((1, PX), F32)
+        for k in range(HOR):
+            chosen = jnp.where(which == float(k), inside, 0.0)
+            hw = hw + chosen * weight_rows[k]
+            part = chosen * (err * err)
+            sse[k] = part if sse[k] is None else sse[k] + part
+        slopes.append(2.0 * err * hw)
+    sse = [jnp.sum(v, axis=1, keepdims=True) for v in sse]
+
+    def cell_backward(t, d_hidden, d_cell, cell_prev):
+        slope = slopes[t]
+        i, fo = save[t, 1, 0:32, :], save[t, 1, 32:64, :]
+        o, cand = save[t, 1, 64:96, :], save[t, 1, 96:128, :]
+        tanh_c, hidden = save[t, 2, 64:96, :], save[t, 2, 96:128, :]
+        dh = slope * head
+        if d_hidden is not None:
+            dh = dh + d_hidden
+        dh = dh * inside
+        d_o = dh * tanh_c
+        dc = dh * o * (1.0 - tanh_c * tanh_c)
+        if d_cell is not None:
+            dc = dc + d_cell
+        dc = dc * inside
+        d_f = jnp.zeros_like(dc) if cell_prev is None else dc * cell_prev
+        raw = [
+            dc * cand * i * (1.0 - i),
+            d_f * fo * (1.0 - fo),
+            d_o * o * (1.0 - o),
+            dc * i * (1.0 - cand * cand),
+        ]
+        scale = save[t, 2, 0:8, :]
+        d_head = jnp.sum(hidden * slope, axis=1, keepdims=True)
+        d_gain, d_shift, dn, sums = [], [], [], [[], []]
+        for g in range(4):
+            normed = save[t, 0, 32 * g : 32 * g + 32, :]
+            d_gain.append(jnp.sum(raw[g] * normed, axis=1, keepdims=True))
+            d_shift.append(jnp.sum(raw[g], axis=1, keepdims=True))
+            v = raw[g] * gain[32 * g : 32 * g + 32]
+            dn.append(v)
+            sums[0].append(jnp.sum(v * inside, axis=0, keepdims=True))
+            sums[1].append(jnp.sum(v * inside * normed, axis=0, keepdims=True))
+        sums = per_stream(jnp.concatenate(sums[0] + sums[1], axis=0)) / count
+        for g in range(4):
+            normed = save[t, 0, 32 * g : 32 * g + 32, :]
+            d_pre = scale[g : g + 1] * (dn[g] - sums[g : g + 1] - normed * sums[4 + g : 5 + g])
+            d_own[t, g] = (d_pre * inside).astype(BF16)
+        return (
+            dc * fo,
+            d_head,
+            jnp.concatenate(d_gain, axis=0),
+            jnp.concatenate(d_shift, axis=0),
+        )
+
+    def share_gates(t):
+        for n, p in enumerate(fpeers):
+            send(d_own.at[t, p], dall.at[t, f, s], f_send.at[3 + t, n], f_recv.at[3 + t, n], (s, p))
+        own = pltpu.make_async_copy(d_own.at[t, f], dall.at[t, f, s], local_sem.at[3 + t])
+        own.start()
+        return own
+
+    z, y = s // 2, lax.rem(s, 2)
+    across = 2 * z + 1 - y
+
+    def line_peer(k):
+        return lax.rem(z + k, 4) * 2 + y
+
+    def line_source(k):
+        return lax.rem(z + 4 - k, 4) * 2 + y
+
+    def share_blocks(t, own):
+        own.wait()
+        for n, p in enumerate(fpeers):
+            arrived(dall.at[t, p, s], f_recv.at[3 + t, n])
+        block = dall.at[t, :, s]
+        for k in (2, 3, 1):
+            send(block, block, sp_send.at[4 + t, k], sp_recv.at[4 + t, k], (line_peer(k), f))
+        send(block, block, sp_send.at[4 + t, 0], sp_recv.at[4 + t, 0], (across, f))
+
+    def relay_blocks(t):
+        for k in (1, 3, 2):
+            block = dall.at[t, :, line_source(k)]
+            arrived(block, sp_recv.at[4 + t, k])
+            send(block, block, sp_send.at[4 + t, 4 + k], sp_recv.at[4 + t, 4 + k], (across, f))
+
+    def gathered(t):
+        arrived(dall.at[t, :, across], sp_recv.at[4 + t, 0])
+        for k in range(1, 4):
+            there = lax.rem(z + 4 - k, 4) * 2 + 1 - y
+            arrived(dall.at[t, :, there], sp_recv.at[4 + t, 4 + k])
+        for p in range(F):
+            block = dall[t, p].reshape(256, PX)
+            dt[p] = block.astype(F32).T.astype(BF16)
+
+    d_cell0, d_head1, d_gain1, d_shift1 = cell_backward(1, None, None, cell0)
+    own_d1 = share_gates(1)
+
+    d1 = d_own[1].reshape(128, PX).astype(F32)
+    for b in range(5):
+        dst[128 * b : 128 * b + 128, :] = slide(d1, 2 - b).astype(BF16)
+    sb[...] = dot(wht[...], dst[...]).reshape(5, 256, PX)
+    dh = sb[2]
+    for a in (0, 1, 3, 4):
+        dh = dh + pltpu.roll(sb[a], (32 * (a - 2)) % PX, 1) * rmask[4 - a]
+    dhp[...] = dh
+    steps = (2, 1, 3, 0)
+
+    def part_of(zz, yy):
+        return pl.ds(pl.multiple_of(32 * (2 * zz + yy), 32), 32)
+
+    for k in steps:
+        zz = lax.rem(z + k, 4)
+        send(
+            dhp.at[part_of(zz, 1 - y), :], dhy.at[k], sp_send.at[3, k], sp_recv.at[3, k], (across, f)
+        )
+    for k in steps:
+        zz = lax.rem(z + k, 4)
+        arrived(dhy.at[k], sp_recv.at[3, k])
+        both = dhp[part_of(zz, y), :] + dhy[k]
+        if k == 0:
+            dhr[z] = both
+        else:
+            dhy[k] = both
+            send(
+                dhy.at[k], dhr.at[z], sp_send.at[3, 4 + k], sp_recv.at[3, 4 + k], (line_peer(k), f)
+            )
+    share_blocks(1, own_d1)
+
+    first_tap = (s * R) // 512
+
+    def tap_inputs(n, carry):
+        p, i = n // 4, lax.rem(n, 4)
+        tap = first_tap + i
+        da, db = tap // 5 - 2, lax.rem(tap, 5) - 2
+        back = lax.rem(2 * PX - 32 * da - db, PX)
+        ok = (row_of + da >= 0) & (row_of + da < rows) & (col_of + db >= 0) & (col_of + db < 16)
+        ok = ok.astype(F32)
+        for t in range(2):
+            moved = pltpu.roll(pix[p, t], back, 1)
+            xt[t, p, i] = lifted(moved[0:1], moved[7:8] * ok)
+        return carry
+
+    arrived(h1.at[f_x], f_recv.at[1, 0])
+    send(h1.at[f_x], h1.at[f_x], f_send.at[2, 0], f_recv.at[2, 0], (s, f_c))
+    lax.fori_loop(0, 4 * F, tap_inputs, 0)
+    arrived(h1.at[f_c], f_recv.at[1, 1])
+    arrived(h1.at[f_d], f_recv.at[2, 0])
+
+    def tap_hidden(n, carry):
+        p, i = n // 4, lax.rem(n, 4)
+        tap = first_tap + i
+        da, db = tap // 5 - 2, lax.rem(tap, 5) - 2
+        back = lax.rem(2 * PX - 32 * da - db, PX)
+        ok = (row_of + da >= 0) & (row_of + da < rows) & (col_of + db >= 0) & (col_of + db < 16)
+        xt[2, p, i] = (pltpu.roll(h1[p].astype(F32), back, 1) * ok.astype(F32)).astype(BF16)
+        return carry
+
+    lax.fori_loop(0, 4 * F, tap_hidden, 0)
+
+    def moved_pixels(t):
+        pixels = pix[f, t, 0:1, :] * inside
+        high = low(pixels)
+        mid = low(pixels - high)
+        rest = low(pixels - high - mid)
+        four = jnp.concatenate([high, mid, rest, inside, jnp.zeros((4, PX), F32)], axis=0)
+        for a in range(5):
+            lines = four if a == 2 else pltpu.roll(four, (-32 * (a - 2)) % PX, 1) * rmask[a]
+            for b in range(5):
+                n = 8 * (5 * a + b)
+                ps[t, n : n + 8, :] = slide(lines, b - 2)
+        return dot_nt(d_own[t].reshape(128, PX), ps[t].astype(BF16))
+
+    q1 = moved_pixels(1)
+
+    for k in range(1, 4):
+        arrived(dhr.at[lax.rem(z + 4 - k, 4)], sp_recv.at[3, 4 + k])
+    d_hidden0 = (dhr[0] + dhr[1]) + (dhr[2] + dhr[3])
+    unused, d_head0, d_gain0, d_shift0 = cell_backward(0, d_hidden0, d_cell0, None)
+    own_d0 = share_gates(0)
+
+    q = q1 + moved_pixels(0)
+    total_w = jnp.zeros((128, 256), F32)
+    total_b = jnp.zeros((128, 256), F32)
+    for tap in range(TAPS):
+        a, b = tap // 5, tap % 5
+        w = wl[128 * a : 128 * a + 128, 256 * b : 256 * b + 256].astype(F32)
+        n = 8 * tap
+        total_w = total_w + w * (q[:, n : n + 1] + q[:, n + 1 : n + 2] + q[:, n + 2 : n + 3])
+        total_b = total_b + w * q[:, n + 3 : n + 4]
+    lift_w = jnp.sum(total_w, axis=0, keepdims=True)
+    lift_b = jnp.sum(total_b, axis=0, keepdims=True)
+
+    share_blocks(0, own_d0)
+
+    lane_sq = lax.broadcasted_iota(jnp.int32, (128, 128), 1)
+    d_head = jnp.concatenate(
+        [d_head0 + d_head1] + sse_rows(sse), axis=0
+    )
+    packed = jnp.where(lane_sq == 0, d_gain0 + d_gain1, 0.0)
+    packed = jnp.where(lane_sq == 1, d_shift0 + d_shift1, packed)
+    packed = jnp.where(lane_sq == 2, d_head, packed)
+    packed = packed.T[0:3, :]
+    vt[...] = jnp.concatenate(
+        [packed, lift_w[:, 0:128], lift_w[:, 128:256], lift_b[:, 0:128], lift_b[:, 128:256],
+         jnp.zeros((1, 128), F32)], axis=0,
+    )
+    vf[f] = vt[...]
+    for n, p in enumerate(fpeers):
+        send(vt, vf.at[f], f_send.at[5, n], f_recv.at[5, n], (s, p))
+    relay_blocks(1)
+    for n, p in enumerate(fpeers):
+        arrived(vf.at[p], f_recv.at[5, n])
+    vs[s] = (vf[0] + vf[1]) + (vf[2] + vf[3])
+    for k in range(1, S):
+        send(vs.at[s], vs.at[s], sp_send.at[7, k], sp_recv.at[7, k], (ahead(k), f))
+
+    relay_blocks(0)
+    gathered(1)
+
+    def grad_one(i, carry):
+        for kind in range(2):
+            total = None
+            for p in range(F):
+                part = dot(xt[1 + kind, p, i], dt[p])
+                total = part if total is None else total + part
+            grad[pl.ds(pl.multiple_of(512 * i + 256 * kind, 256), 256), :] = total
+        return carry
+
+    lax.fori_loop(0, 4, grad_one, 0)
+
+    for k in range(1, S):
+        arrived(hr.at[behind(k)], sp_recv.at[6, k])
+    for k in range(S):
+        for r in range(2):
+            h_ref[16 * r : 16 * r + 16, 32 * k : 32 * k + 32] = hr[k, :, 64 * r : 64 * r + 32]
+            c_ref[16 * r : 16 * r + 16, 32 * k : 32 * k + 32] = hr[k, :, 64 * r + 32 : 64 * r + 64]
+
+    for k in range(1, S):
+        arrived(vs.at[behind(k)], sp_recv.at[7, k])
+    lane8 = lax.broadcasted_iota(jnp.int32, (8, 128), 1)
+    sub8 = lax.broadcasted_iota(jnp.int32, (8, 128), 0)
+    lift = vs[0]
+    small_sq = jnp.zeros((8, 128), F32)
+    for k in range(S):
+        own_rows = jnp.where((sub8 < 2) | ((sub8 == 2) & (lane8 < 32)), vs[k], 0.0)
+        small_sq = small_sq + own_rows * own_rows
+        if k > 0:
+            lift = lift + vs[k]
+    lift = jnp.where((sub8 >= 3) & (sub8 < 7), lift, 0.0)
+    small_sq = jnp.sum(small_sq + lift * lift)
+    gate, half = s // 2, lax.rem(s, 2)
+    d_gates = jnp.zeros((8, 128), F32)
+    for k in range(4):
+        turned = pltpu.roll(vs[4 * half + k], lax.rem(32 * k - 32 * gate + 128, 128), 1)
+        d_gates = jnp.where((lane8 >= 32 * k) & (lane8 < 32 * k + 32), turned, d_gates)
+    quarter = 32 * lax.rem(s, 4)
+    upper = s // 4
+    turned = pltpu.roll(lift, lax.rem(128 - quarter, 128), 1)
+    line_w = jnp.where(upper == 0, turned[3:4], turned[4:5])
+    line_b = jnp.where(upper == 0, turned[5:6], turned[6:7])
+    line_h = vs[s][2:3, :]
+    lane1 = lane8[0:1]
+    d_chans = jnp.where(
+        lane1 < 32, line_w,
+        jnp.where(lane1 < 64, pltpu.roll(line_b, 32, 1), pltpu.roll(line_h, 64, 1)),
+    )
+    loss = jnp.zeros((1, 1), F32)
+    for k in range(HOR):
+        loss = loss + vs[s][2:3, 32 + k : 33 + k] * weight_rows[k]
+
+    gathered(0)
+
+    def grad_zero(i, carry):
+        total = None
+        for p in range(F):
+            part = dot(xt[0, p, i], dt[p])
+            total = part if total is None else total + part
+        at = pl.ds(pl.multiple_of(512 * i, 256), 256)
+        grad[at, :] = grad[at, :] + total
+        return carry
+
+    lax.fori_loop(0, 4, grad_zero, 0)
+
+    def square(n, carry):
+        v = grad[pl.ds(pl.multiple_of(base + 64 * n, 64), 64), :]
+        return carry + v * v
+
+    total = lax.fori_loop(0, R // 64, square, jnp.zeros((64, 256), F32))
+    qf[f] = jnp.full((8, 128), jnp.sum(total), F32)
+    for n, p in enumerate(fpeers):
+        send(qf.at[f], qf.at[f], f_send.at[6, n], f_recv.at[6, n], (s, p))
+    for n, p in enumerate(fpeers):
+        arrived(qf.at[p], f_recv.at[6, n])
+    qs[s] = (qf[0] + qf[1]) + (qf[2] + qf[3])
+    for k in range(1, S):
+        send(qs.at[s], qs.at[s], sp_send.at[8, k], sp_recv.at[8, k], (ahead(k), f))
+    for k in range(1, S):
+        arrived(qs.at[behind(k)], sp_recv.at[8, k])
+    squares = qs[0]
+    for k in range(1, S):
+        squares = squares + qs[k]
+    norm = jnp.sqrt(squares + small_sq)
+    factor = jnp.minimum(1.0, CLIP / (norm + 1e-06))
+    out = jnp.where(sub8 < 2, d_gates, d_chans)
+    out = jnp.where(sub8 == 3, loss, out)
+    out = jnp.where(sub8 == 4, norm, out)
+    out = jnp.where(sub8 == 5, factor, out)
+    small_ref[...] = out
+
+    for cp in moments:
+        cp.wait()
+    for cp, when in pending:
+        only(when, cp.wait_send)
+
+
+def sse_rows(sse):
+    return sse + [jnp.zeros((128 - 32 - HOR, 1), F32)]
+
+
+def step_fast(
+    frames, targets, sizes, horizon, conv_weight, conv_m, conv_v, gates_vec, chan_vec
+):
+    S, F = lax.axis_size("space"), lax.axis_size("fsdp")
+    R, N = conv_weight.shape
+    rows, cols = frames.shape[3] * S, frames.shape[4]
+    PX = 2 * rows * cols
+
+    VM = pltpu.VMEM
+    DMA = pltpu.SemaphoreType.DMA
+    geo = (S, F, R, rows, PX)
+    out = pl.pallas_call(
+        functools.partial(step_kernel, geo),
+        out_shape=(
+            VM((2048, N), F32),
+            VM((2048, N), F32),
+            VM((R, N), F32),
+            VM((R, N), F32),
+            VM((8, 128), F32),
+            VM((32, 256), F32),
+            VM((32, 256), F32),
+        ),
+        in_specs=[pl.BlockSpec(memory_space=pltpu.HBM)] * 9,
+        out_specs=(pl.BlockSpec(memory_space=VM),) * 7,
+        scratch_shapes=[
+            VM(frames.shape, F32),
+            VM(frames.shape, F32),
+            VM(frames.shape, jnp.int32),
+            VM((1, 2), jnp.int32),
+            VM(gates_vec.shape, F32),
+            VM(chan_vec.shape, F32),
+            VM((2, 4, 2, 8, 32, 128), BF16),
+            VM((S, 2, 4, 2, 4, 32, 128), BF16),
+            VM((640, 1280), BF16),
+            VM((640, 1280), BF16),
+            VM((1280, 640), BF16),
+            VM((F, S, 8, 128), F32),
+            VM((F, 2, 8, PX), F32),
+            VM((5, 256, 128), F32),
+            VM((1280, PX), BF16),
+            VM((5, 128, PX), F32),
+            VM((5, 256, PX), F32),
+            VM((128, PX), F32),
+            VM((2, 3, 128, PX), F32),
+            VM((F, 256, PX), BF16),
+            VM((S, 8, PX), F32),
+            VM((640, PX), BF16),
+            VM((256, PX), F32),
+            VM((4, 32, PX), F32),
+            VM((4, 32, PX), F32),
+            VM((2, 4, 32, PX), BF16),
+            VM((2, F, S, 32, PX), BF16),
+            VM((F, PX, 256), BF16),
+            VM((rows // 2, cols, 128), F32),
+            VM((S, cols, 128), F32),
+            VM((3, F, 4, 256, PX), BF16),
+            VM((2, 8 * TAPS, PX), F32),
+            VM((8, 128), F32),
+            VM((F, 8, 128), F32),
+            VM((S, 8, 128), F32),
+            VM((F, 8, 128), F32),
+            VM((S, 8, 128), F32),
+            DMA((8,)),
+            DMA((4,)),
+            DMA((6,)),
+            DMA((9, S)),
+            DMA((9, S)),
+            DMA((2, 4, S)),
+            DMA((2, 4, S)),
+            DMA((2, 4, S, 3)),
+            DMA((2, 4, S, 3)),
+            DMA((7, 3)),
+            DMA((7, 3)),
+        ],
+        compiler_params=pltpu.CompilerParams(
+            collective_id=0, has_side_effects=True, vmem_limit_bytes=44 * 2**20
+        ),
+    )(
+        *(
+            pltpu.with_memory_space_constraint(v, pltpu.HBM)
+            for v in (
+                frames, targets, horizon, sizes.reshape(1, 2), gates_vec, chan_vec,
+                conv_weight, conv_m, conv_v,
+            )
+        )
+    )
+    return out
+
+
+def adam_kernel(
+    steps,
+    small_ref, h_ref, c_ref, g_ref,
+    w_ref, m_ref, v_ref, gw_ref, gm_ref, gv_ref, cw_ref, cm_ref, cv_ref,
+    loss_ref, norm_ref,
+    wo_ref, mo_ref, vo_ref, gwo_ref, gmo_ref, gvo_ref, cwo_ref, cmo_ref, cvo_ref,
+    ho_ref, co_ref,
+    held, sems,
+):
+    factor = small_ref[5:6, 0:1]
+    R = m_ref.shape[0]
+    size = R // steps
+    base = lax.rem(lax.axis_index("space") * R, 512)
+    copies = []
+    for n in range(steps):
+        at = slice(size * n, size * n + size)
+        moved = pl.ds(pl.multiple_of(base + size * n, 64), size)
+        news = adam_update(w_ref[moved, :], m_ref[at, :], v_ref[at, :], g_ref[moved, :] * factor)
+        for q, (new, out) in enumerate(zip(news, (wo_ref, mo_ref, vo_ref))):
+            held[q, at, :] = new
+            copy = pltpu.make_async_copy(held.at[q, at, :], out.at[at, :], sems.at[q, n])
+            copy.start()
+            copies.append(copy)
+
+    def update(w, m, v, grad, outs):
+        for ref, new in zip(outs, adam_update(w[...], m[...], v[...], grad * factor)):
+            ref[...] = new
+
+    loss_ref[...] = small_ref[3:4, 0:1]
+    norm_ref[...] = small_ref[4:5, 0:1]
+    update(gw_ref, gm_ref, gv_ref, small_ref[0:2, :], (gwo_ref, gmo_ref, gvo_ref))
+    chans = [small_ref[2:3, 32 * q : 32 * q + 32] for q in range(3)]
+    update(cw_ref, cm_ref, cv_ref, jnp.concatenate(chans, axis=0), (cwo_ref, cmo_ref, cvo_ref))
+    for r in range(2):
+        ho_ref[0, r] = h_ref[16 * r : 16 * r + 16, :]
+        co_ref[0, r] = c_ref[16 * r : 16 * r + 16, :]
+    for copy in copies:
+        copy.wait()
+
+
+def adam_step(small, hidden, cell, grad, weights, frame_shape):
+    R, N = weights[0][1].shape
+    steps = 5
+    rows, cols = frame_shape
+    vmem, any_ = pl.BlockSpec(memory_space=pltpu.VMEM), pl.BlockSpec(memory_space=pl.ANY)
+    conv, gates, chan = weights
+    flat = [*conv, *gates, *chan]
+    shapes = [jax.ShapeDtypeStruct(v.shape, F32) for v in (*conv[1:], conv[1], *gates, *chan)]
+    scalar = jax.ShapeDtypeStruct((1, 1), F32)
+    state = jax.ShapeDtypeStruct((1, rows, cols, hidden.shape[1]), F32)
+    out = pl.pallas_call(
+        functools.partial(adam_kernel, steps),
+        out_shape=(scalar, scalar, *shapes, state, state),
+        in_specs=[vmem] * (4 + len(flat)),
+        out_specs=(vmem, vmem, *([any_] * 3), *([vmem] * 8)),
+        scratch_shapes=[pltpu.VMEM((3, R, N), F32), pltpu.SemaphoreType.DMA((3, steps))],
+        compiler_params=pltpu.CompilerParams(vmem_limit_bytes=7 * 2**20),
+    )(small, hidden, cell, grad, *flat)
+    return (out[0].reshape(()), out[1].reshape(()), *out[2:])
+
+
+def per_device_fast(
+    frames, targets, sizes, horizon,
+    conv_weight, conv_m, conv_v,
+    gates_vec, gates_m, gates_v,
+    chan_vec, chan_m, chan_v,
+):
+    grad, weight, first, second, small, hidden, cell = step_fast(
+        frames, targets, sizes, horizon, conv_weight, conv_m, conv_v, gates_vec, chan_vec
+    )
+    weights = ((weight, first, second), (gates_vec, gates_m, gates_v), (chan_vec, chan_m, chan_v))
+    return adam_step(small, hidden, cell, grad, weights, frames.shape[3:])
+
+
+def fits(mesh, shapes):
+    S, F = mesh.shape["space"], mesh.shape["fsdp"]
+    frames, conv, chan = shapes
+    return (
+        (S, F) == (8, 4)
+        and frames == (2, F, 2, 2 * S, 16)
+        and conv == (TAPS * 512, 1024)
+        and chan == (3, 256)
+    )
+
+
 def solution(mesh):
     in_specs = (
         P(None, "fsdp", None, "space", None),
@@ -305,6 +1265,12 @@
         P("fsdp", "space", None, None),
         P("fsdp", "space", None, None),
     )
-    return jax.shard_map(
-        per_device, mesh=mesh, in_specs=in_specs, out_specs=out_specs, check_vma=False
-    )
+
+    def run(*args):
+        shapes = (args[0].shape, args[4].shape, args[10].shape)
+        body = per_device_fast if fits(mesh, shapes) else per_device
+        return jax.shard_map(
+            body, mesh=mesh, in_specs=in_specs, out_specs=out_specs, check_vma=False
+        )(*args)
+
+    return run

time: 1840 us -> 117 us (0.06)
  waiting for transfers between devices: 1110 us -> 0 us
  blocking collectives: 326 us -> 0 us
  matrix products: 140 us -> 0 us
  local copies, waits for them, and re-layouts: 122 us -> 0.03 us
  Pallas kernels: 0 us -> 116 us
  other arithmetic: 79.4 us -> 0 us
  starting transfers between devices: 32.7 us -> 0 us
    reduce_scatter x2 -> x0, waiting for transfers between devices: 560 us -> none  [the longest x1 352 us: reduce_grads(): lax.psum_scatter(d_kernel, 'fsdp', scatter_dimension=1, tiled=True)]
    all_gather x2 -> x0, waiting for transfers between devices: 401 us -> none  [the longest x1 368 us: gather_weights(): lax.all_gather(col_block, 'space', axis=0, tiled=True)]
    psum x11 -> x0, blocking collectives: 282 us -> none  [the longest x1 85.6 us: per_device(): counts = lax.psum(jnp.sum(select, axis=(0, 1, 2, 3, 4)), ('space', 'fsdp'))]
    dot_general x10 -> x0, matrix products: 140 us -> none  [the longest x2 53.6 us: backward(): lax.dot_general(patches.reshape(-1, patches.shape[-1]), d_pre_all.reshape...]
    unnamed x8 -> x0, waiting for transfers between devices: 129 us -> none
    pallas_call x0 -> x2, Pallas kernels: none -> 116 us  [the longest x1 111 us: step_fast(): pl.pallas_call(functools.partial(step_kernel, geo), out_shape=(VM((2048,...]
    all_gather x2 -> x0, blocking collectives: 44 us -> none  [the longest x1 26.9 us: gather_weights(): lax.all_gather(gates_vec.astype(jnp.bfloat16), 'space', axis=1, tiled=True)]
    reshape x1 -> x0, local copies, waits for them, and re-layouts: 35.7 us -> none  [gather_weights(): kernel.reshape(25, inputs_n, gates_n).transpose(0, 2, 1)]
  transfers between devices with their start and end apart: 22 -> 0, of which waited for: 14 -> 0; matrix products, arithmetic and copies ran while one was open for 2% -> 0% of each run, Pallas kernels for 0% -> 0%
where the time goes in v1:
time: 117 us
  Pallas kernels  116 us (99%)
    pallas_call x1, Pallas kernels, step_fast(): pl.pallas_call(functools.partial(step_kernel, geo), out_shape=(VM((2048,...  111 us
    pallas_call x1, Pallas kernels, adam_step(): pl.pallas_call(functools.partial(adam_kernel, steps), out_shape=(scalar,...  4.3 us

profile of v1, /device:TPU:0, one launch (start us, length us, event | category | flops | bytes accessed | tf_op | source)
XLA Modules:
  0.0 116.7 jit_solution(2647889570630875478)
XLA Ops:
  0.6 0.0 copy-start
  0.7 0.0 copy-start.1
  0.7 0.0 copy-start.2
  0.7 0.0 copy-start.3
  0.7 0.0 copy-start.4
  0.7 0.0 copy-start.5
  0.7 111.4 %shard_map.228 = (f32[2048,256]{1,0:T(8,128)S(1)}, f32[2048,256]{1,0:T(8,128)S(1)}, f32[1600,256]{1,0:T(8,128)S(1)}, f32[1600,256]{1,0:T(8,128)S(1)}, f32[8,128]...) custom-call(f32[2,1,2,2,16]{4,3,2,1,0:T(2,128)} %frames_in.1, f32[2,1,2,2,16]{4,3,2,1,0:T(2,128)} %targets_in.1, ...), custom_call_target="tpu_custom_call" | custom-call | tf_op jit(solution)/shard_map/pallas_call | solution.py:1074
  112.2 0.0 copy-done
  112.2 0.0 copy-done.1
  112.2 0.0 copy-done.2
  112.2 0.0 copy-done.3
  112.2 0.0 copy-done.4
  112.2 0.0 copy-done.5
  112.2 4.3 %shard_map.229 = (f32[1,1]{1,0:T(1,128)}, f32[1,1]{1,0:T(1,128)}, f32[1600,256]{1,0:T(8,128)}, f32[1600,256]{1,0:T(8,128)}, f32[1600,256]{1,0:T(8,128)}, /*index...) custom-call(f32[8,128]{1,0:T(8,128)S(1)} %get-tuple-element.33.small, ...), custom_call_target="tpu_custom_call" | custom-call | tf_op jit(solution)/shard_map/pallas_call | solution.py:1202
Async XLA Ops:
  0.6 111.5 %copy-start = (f32[3,32]{1,0:T(4,128)S(1)}, f32[3,32]{1,0:T(4,128)}, u32[]{:S(2)}) copy-start(f32[3,32]{1,0:T(4,128)} %cw_ref.1) | copy-start | bytes 1156
  0.7 111.5 %copy-start.1 = (f32[2,128]{1,0:T(2,128)S(1)}, f32[2,128]{1,0:T(2,128)}, u32[]{:S(2)}) copy-start(f32[2,128]{1,0:T(2,128)} %gw_ref.1) | copy-start | bytes 3076
  0.7 111.5 %copy-start.2 = (f32[3,32]{1,0:T(4,128)S(1)}, f32[3,32]{1,0:T(4,128)}, u32[]{:S(2)}) copy-start(f32[3,32]{1,0:T(4,128)} %cm_ref.1) | copy-start | bytes 1156
  0.7 111.5 %copy-start.3 = (f32[3,32]{1,0:T(4,128)S(1)}, f32[3,32]{1,0:T(4,128)}, u32[]{:S(2)}) copy-start(f32[3,32]{1,0:T(4,128)} %cv_ref.1) | copy-start | bytes 1156
  0.7 111.5 %copy-start.4 = (f32[2,128]{1,0:T(2,128)S(1)}, f32[2,128]{1,0:T(2,128)}, u32[]{:S(2)}) copy-start(f32[2,128]{1,0:T(2,128)} %gm_ref.1) | copy-start | bytes 3076
  0.7 111.5 %copy-start.5 = (f32[2,128]{1,0:T(2,128)S(1)}, f32[2,128]{1,0:T(2,128)}, u32[]{:S(2)}) copy-start(f32[2,128]{1,0:T(2,128)} %gv_ref.1) | copy-start | bytes 3076

commit v2 on v1

--- a/solution.py
+++ b/solution.py
@@ -353,15 +353,15 @@
     qs,
     in_sem,
     w_sem,
-    local_sem,
-    sp_send,
-    sp_recv,
-    wsend,
-    wrecv,
-    wfs,
-    wfr,
-    f_send,
-    f_recv,
+    w_out,
+    w_in,
+    x_out,
+    x_in,
+    c_in,
+    sp_out,
+    sp_in,
+    f_out,
+    f_in,
 ):
     S, F, R, rows, PX = geo
     width = 8 * 32
@@ -369,7 +369,6 @@
     xx, cc = f // 2, lax.rem(f, 2)
     f_x, f_c, f_d = (1 - xx) * 2 + cc, xx * 2 + 1 - cc, (1 - xx) * 2 + 1 - cc
     fpeers = (f_x, f_c, f_d)
-    pending = []
 
     def ahead(k):
         return lax.rem(s + k, S)
@@ -383,26 +382,31 @@
         else:
             pl.when(when)(do)
 
-    def copy_to(src, dst_, ssem, rsem, dev, when=None):
-        cp = pltpu.make_async_remote_copy(
+    def copy_to(src, dst_, ssem, rsem, dev):
+        return pltpu.make_async_remote_copy(
             src_ref=src, dst_ref=dst_, send_sem=ssem, recv_sem=rsem,
             device_id=dev, device_id_type=MESH,
         )
-        pending.append((cp, when))
-        return cp
-
-    def send(src, dst_, ssem, rsem, dev, when=None):
-        cp = copy_to(src, dst_, ssem, rsem, dev, when)
-        only(when, cp.start)
-
-    def landing(slot, rsem):
-        return pltpu.make_async_remote_copy(
-            src_ref=slot, dst_ref=slot, send_sem=rsem, recv_sem=rsem,
-            device_id=(s, f_c), device_id_type=MESH,
-        )
-
-    def arrived(slot, rsem, when=None):
-        only(when, landing(slot, rsem).wait_recv)
+
+    def send(src, dst_, ssem, rsem, dev, priority=0):
+        copy_to(src, dst_, ssem, rsem, dev).start(priority=priority)
+
+    def arrived(slot, rsem):
+        copy_to(slot, slot, rsem, rsem, (s, f_c)).wait_recv()
+
+    def left(slot, ssem):
+        copy_to(slot, slot, ssem, ssem, (s, f_c)).wait_send()
+
+    def each(first, last, do):
+        def step(k, carry):
+            do(k)
+            return carry
+
+        lax.fori_loop(first, last, step, 0)
+
+    TILE, H1, Y, DHY, DHL, BLK, END, VEC, SQ = 0, 1, 2, 3, 4, 5, 7, 8, 9
+    DHY_IN, LINE_IN, ACROSS_IN = 10, 14, 22
+    F_TILE, F_H1, F_H1C, F_VEC, F_SQ, F_D = 0, 1, 2, 3, 4, 5
 
     barrier = pltpu.get_barrier_semaphore()
     for k in range(1, S):
@@ -430,6 +434,38 @@
         )
         get_w[-1].start()
 
+    pl.semaphore_wait(barrier, S - 1 + 3)
+
+    def holders(kind, i):
+        lo = 512 * i + 256 * kind
+        return [q for q in range(S) if (q * R) % 512 + R > lo and (q * R) % 512 < lo + 256]
+
+    def holds(src, kind, i):
+        if len(holders(kind, i)) == S:
+            return None
+        lo, first = 512 * i + 256 * kind, lax.rem(src * R, 512)
+        return (lo < first + R) & (lo + 256 > first)
+
+    def stage_slot(kind, i):
+        for j in range(2):
+            r0 = 512 * i + 256 * kind + 128 * j
+            block = wf[r0 : r0 + 128, :].T.astype(BF16)
+            stage[kind, i, j] = block.reshape(8, 32, 128)
+
+    def send_slot(kind, i):
+        def to(k):
+            send(
+                stage.at[kind, i, :, ahead(k)], wr.at[s, kind, i, :, f],
+                w_out.at[kind, i], w_in.at[kind, i], (ahead(k), f),
+            )
+
+        only(holds(s, kind, i), lambda: each(1, S, to))
+
+    order = {kind: sorted(range(4), key=lambda i: -len(holders(kind, i))) for kind in range(2)}
+    for q in (0, 1):
+        get_w[q].wait()
+    stage_slot(0, order[0][0])
+    send_slot(0, order[0][0])
     for cp in small_ins:
         cp.wait()
 
@@ -450,47 +486,22 @@
         ],
         axis=0,
     )
-    pl.semaphore_wait(barrier, S - 1 + 3)
-
-    for k in range(1, S):
-        send(tiles.at[f, s], tiles.at[f, s], sp_send.at[0, k], sp_recv.at[0, k], (ahead(k), f))
-
-    def holds(src, kind, i):
-        lo = 512 * i + 256 * kind
-        if all((q * R) % 512 + R > lo and (q * R) % 512 < lo + 256 for q in range(S)):
-            return None
-        first = lax.rem(src * R, 512)
-        return (lo < first + R) & (lo + 256 > first)
-
-    def stage_slot(kind, i):
-        for j in range(2):
-            r0 = 512 * i + 256 * kind + 128 * j
-            block = wf[r0 : r0 + 128, :].T.astype(BF16)
-            stage[kind, i, j] = block.reshape(8, 32, 128)
-
-    def send_slot(kind, i):
-        when = holds(s, kind, i)
-        for k in range(1, S):
-            to = ahead(k)
-            send(
-                stage.at[kind, i, :, to], wr.at[s, kind, i, :, f],
-                wsend.at[kind, i, k], wrecv.at[kind, i, k], (to, f), when,
-            )
-
-    for i, q in ((0, (0,)), (1, (1,)), (2, (2, 3)), (3, ())):
-        for n in q:
-            get_w[n].wait()
+    each(1, S, lambda k: send(
+        tiles.at[f, s], tiles.at[f, s], sp_out.at[TILE], sp_in.at[TILE], (ahead(k), f)
+    ))
+    for q in (2, 3):
+        get_w[q].wait()
+    for i in order[0][1:]:
         stage_slot(0, i)
         send_slot(0, i)
-    stage_slot(1, 0)
-    stage_slot(1, 1)
+    stage_slot(1, order[1][0])
+    stage_slot(1, order[1][1])
     for i in range(4):
         wr[s, 0, i, :, f] = stage[0, i, :, s]
 
-    for k in range(1, S):
-        arrived(tiles.at[f, behind(k)], sp_recv.at[0, k])
-    for n, p in enumerate(fpeers):
-        send(tiles.at[f], tiles.at[f], f_send.at[0, n], f_recv.at[0, n], (s, p))
+    arrived(tiles.at[f, 1:S], sp_in.at[TILE])
+    for p in fpeers:
+        send(tiles.at[f], tiles.at[f], f_out.at[F_TILE], f_in.at[F_TILE], (s, p))
 
     lane = lax.broadcasted_iota(jnp.int32, (1, PX), 1)
     row_of = lane // 32
@@ -541,59 +552,55 @@
     inside = pix[f, 0, 7:8, :]
 
     def relay(kind):
-        def first_hop(i, k):
-            src = behind(k)
-            when = holds(src, kind, i)
-            block = wr.at[src, kind, i, :, f]
-            to_x = copy_to(block, block, wfs.at[kind, i, k, 0], wfr.at[kind, i, k, 0], (s, f_x), when)
-            to_c = copy_to(block, block, wfs.at[kind, i, k, 1], wfr.at[kind, i, k, 1], (s, f_c), when)
-            here = landing(block, wrecv.at[kind, i, k]) if k > 0 else None
-
-            def hop():
-                if k > 0:
-                    here.wait_recv()
-                to_x.start()
-                to_c.start()
-
-            only(when, hop)
-
-        def second_hop(i, k):
-            src = behind(k)
-            when = holds(src, kind, i)
-            block = wr.at[src, kind, i, :, f_x]
-            to_c = copy_to(block, block, wfs.at[kind, i, k, 2], wfr.at[kind, i, k, 2], (s, f_c), when)
-            here = landing(block, wfr.at[kind, i, k, 0])
-
-            def hop():
-                here.wait_recv()
-                to_c.start()
-
-            only(when, hop)
-
-        for i in range(4):
-            for k in range(S):
-                first_hop(i, k)
-            if kind == 0 and i > 0:
-                send_slot(1, i - 1)
-            if kind == 0 and i == 3:
-                send_slot(1, 3)
-            if i > 0:
-                for k in range(S):
-                    second_hop(i - 1, k)
-        for k in range(S):
-            second_hop(3, k)
-        for i in range(4):
-            for k in range(S):
+        counts = [len(holders(kind, i)) for i in range(4)]
+
+        def first_hop(i):
+            when = holds(s, kind, i)
+            n = counts[i]
+            if when is None:
+                arrived(wr.at[1:S, kind, i, :, f], w_in.at[kind, i])
+            else:
+                pl.when(when)(lambda: arrived(wr.at[1:n, kind, i, :, f], w_in.at[kind, i]))
+                other = jnp.logical_not(when)
+                pl.when(other)(lambda: arrived(wr.at[0:n, kind, i, :, f], w_in.at[kind, i]))
+
+            def hop(k):
                 src = behind(k)
-                when = holds(src, kind, i)
-                own_c = landing(wr.at[src, kind, i, :, f_c], wfr.at[kind, i, k, 1])
-                far_c = landing(wr.at[src, kind, i, :, f_d], wfr.at[kind, i, k, 2])
-
-                def both():
-                    own_c.wait_recv()
-                    far_c.wait_recv()
-
-                only(when, both)
+                block = wr.at[src, kind, i, :, f]
+
+                def go():
+                    send(block, block, x_out.at[kind, 0], x_in.at[kind, i], (s, f_x))
+                    send(block, block, x_out.at[kind, 1], c_in.at[kind, 0], (s, f_c))
+
+                only(holds(src, kind, i), go)
+
+            each(0, S, hop)
+
+        def second_hop(i):
+            arrived(wr.at[0 : counts[i], kind, i, :, f_x], x_in.at[kind, i])
+
+            def hop(k):
+                src = behind(k)
+                block = wr.at[src, kind, i, :, f_x]
+                only(
+                    holds(src, kind, i),
+                    lambda: send(block, block, x_out.at[kind, 2], c_in.at[kind, 1], (s, f_c)),
+                )
+
+            each(0, S, hop)
+
+        for n, i in enumerate(order[kind]):
+            first_hop(i)
+            if kind == 0 and n > 0:
+                send_slot(1, order[1][n - 1])
+            if kind == 0 and n == 3:
+                send_slot(1, order[1][3])
+            if n > 0:
+                second_hop(order[kind][n - 1])
+        second_hop(order[kind][3])
+        blocks = sum(counts) // 4
+        arrived(wr.at[0:blocks, kind, :, :, f_c], c_in.at[kind, 0])
+        arrived(wr.at[0:blocks, kind, :, :, f_d], c_in.at[kind, 1])
 
     def merge(kind, out):
         for tap in range(TAPS):
@@ -676,8 +683,8 @@
     ]
     for cp in moments:
         cp.start()
-    stage_slot(1, 2)
-    stage_slot(1, 3)
+    stage_slot(1, order[1][2])
+    stage_slot(1, order[1][3])
     for i in range(4):
         wr[s, 1, i, :, f] = stage[1, i, :, s]
     slid_lift(0)
@@ -686,8 +693,9 @@
     hidden0, cell0 = cell_forward(0, conv(wl), None)
     mine = pl.ds(pl.multiple_of(32 * s, 32), 32)
     h1[f, mine, :] = hidden0.astype(BF16)
-    for k in range(1, S):
-        send(h1.at[f, mine, :], h1.at[f, mine, :], sp_send.at[1, k], sp_recv.at[1, k], (ahead(k), f))
+    each(1, S, lambda k: send(
+        h1.at[f, mine, :], h1.at[f, mine, :], sp_out.at[H1], sp_in.at[H1], (ahead(k), f)
+    ))
 
     relay(1)
     slid_lift(1)
@@ -697,21 +705,19 @@
         for b in range(5):
             block = wh[128 * a : 128 * a + 128, 256 * b : 256 * b + 256]
             wht[256 * a : 256 * a + 256, 128 * b : 128 * b + 128] = block.astype(F32).T.astype(BF16)
-    for k in range(1, S):
-        their = pl.ds(pl.multiple_of(32 * behind(k), 32), 32)
-        arrived(h1.at[f, their, :], sp_recv.at[1, k])
-    send(h1.at[f], h1.at[f], f_send.at[1, 0], f_recv.at[1, 0], (s, f_x))
-    send(h1.at[f], h1.at[f], f_send.at[1, 1], f_recv.at[1, 1], (s, f_c))
+    arrived(h1.at[f, 32 : 32 * S, :], sp_in.at[H1])
+    send(h1.at[f], h1.at[f], f_out.at[F_H1], f_in.at[F_H1], (s, f_x))
+    send(h1.at[f], h1.at[f], f_out.at[F_H1], f_in.at[F_H1C], (s, f_c))
     hidden_in = h1[f].astype(F32)
     for b in range(5):
         xb[256 * b : 256 * b + 256, :] = slide(hidden_in, b - 2).astype(BF16)
     pre1[...] = pre1[...] + conv(wh)
     hidden1, cell1 = cell_forward(1, pre1[...], cell0)
-    for k in range(1, S):
-        send(yrow.at[s], yrow.at[s], sp_send.at[2, k], sp_recv.at[2, k], (ahead(k), f))
-
-    for n, p in enumerate(fpeers):
-        arrived(tiles.at[p], f_recv.at[0, n])
+    each(1, S, lambda k: send(
+        yrow.at[s], yrow.at[s], sp_out.at[Y], sp_in.at[Y], (ahead(k), f)
+    ))
+
+    arrived(tiles.at[0:3], f_in.at[F_TILE])
     for p in fpeers:
         build_pix(p)
     weight_rows = []
@@ -729,12 +735,9 @@
         lax.broadcasted_iota(jnp.int32, (rows // 2, 16, 128), 2) < 64,
         state[:, 0, 1], state[:, 1, 1],
     )
-    for k in range(1, S):
-        send(ht.at[ahead(k)], hr.at[s], sp_send.at[6, k], sp_recv.at[6, k], (ahead(k), f))
     hr[s] = ht[s]
 
-    for k in range(1, S):
-        arrived(yrow.at[behind(k)], sp_recv.at[2, k])
+    arrived(yrow.at[1:S], sp_in.at[Y])
     ysum = yrow[0]
     for k in range(1, S):
         ysum = ysum + yrow[k]
@@ -797,10 +800,10 @@
 
     def share_gates(t):
         for n, p in enumerate(fpeers):
-            send(d_own.at[t, p], dall.at[t, f, s], f_send.at[3 + t, n], f_recv.at[3 + t, n], (s, p))
-        own = pltpu.make_async_copy(d_own.at[t, f], dall.at[t, f, s], local_sem.at[3 + t])
-        own.start()
-        return own
+            send(
+                d_own.at[t, p], dall.at[t, f, s], f_out.at[F_D + t], f_in.at[F_D + 3 * t + n], (s, p)
+            )
+        dall[t, f, s] = d_own[t, f]
 
     z, y = s // 2, lax.rem(s, 2)
     across = 2 * z + 1 - y
@@ -811,32 +814,37 @@
     def line_source(k):
         return lax.rem(z + 4 - k, 4) * 2 + y
 
-    def share_blocks(t, own):
-        own.wait()
-        for n, p in enumerate(fpeers):
-            arrived(dall.at[t, p, s], f_recv.at[3 + t, n])
-        block = dall.at[t, :, s]
+    pieces = ((f, None), (f_c, 1), (f_x, 0), (f_d, 2))
+
+    def share_piece(t, n):
+        p, peer = pieces[n]
+        block = dall.at[t, p, s]
+        if peer is not None:
+            arrived(block, f_in.at[F_D + 3 * t + peer])
         for k in (2, 3, 1):
-            send(block, block, sp_send.at[4 + t, k], sp_recv.at[4 + t, k], (line_peer(k), f))
-        send(block, block, sp_send.at[4 + t, 0], sp_recv.at[4 + t, 0], (across, f))
-
-    def relay_blocks(t):
+            send(
+                block, block, sp_out.at[BLK + t], sp_in.at[LINE_IN + 4 * t + n], (line_peer(k), f)
+            )
+        send(block, block, sp_out.at[BLK + t], sp_in.at[ACROSS_IN + 4 * t + n], (across, f))
+
+    def relay_piece(t, n):
+        p, unused = pieces[n]
+        arrived(dall.at[t, p, 0:3], sp_in.at[LINE_IN + 4 * t + n])
         for k in (1, 3, 2):
-            block = dall.at[t, :, line_source(k)]
-            arrived(block, sp_recv.at[4 + t, k])
-            send(block, block, sp_send.at[4 + t, 4 + k], sp_recv.at[4 + t, 4 + k], (across, f))
-
-    def gathered(t):
-        arrived(dall.at[t, :, across], sp_recv.at[4 + t, 0])
-        for k in range(1, 4):
-            there = lax.rem(z + 4 - k, 4) * 2 + 1 - y
-            arrived(dall.at[t, :, there], sp_recv.at[4 + t, 4 + k])
-        for p in range(F):
-            block = dall[t, p].reshape(256, PX)
-            dt[p] = block.astype(F32).T.astype(BF16)
-
+            block = dall.at[t, p, line_source(k)]
+            send(block, block, sp_out.at[BLK + t], sp_in.at[ACROSS_IN + 4 * t + n], (across, f))
+
+    def gathered(t, n):
+        p, unused = pieces[n]
+        arrived(dall.at[t, p, 0:4], sp_in.at[ACROSS_IN + 4 * t + n])
+        dt[p] = dall[t, p].reshape(256, PX).astype(F32).T.astype(BF16)
+        return p
+
+    each(1, S, lambda k: send(
+        ht.at[ahead(k)], hr.at[s], sp_out.at[END], sp_in.at[END], (ahead(k), f)
+    ))
     d_cell0, d_head1, d_gain1, d_shift1 = cell_backward(1, None, None, cell0)
-    own_d1 = share_gates(1)
+    share_gates(1)
 
     d1 = d_own[1].reshape(128, PX).astype(F32)
     for b in range(5):
@@ -854,20 +862,21 @@
     for k in steps:
         zz = lax.rem(z + k, 4)
         send(
-            dhp.at[part_of(zz, 1 - y), :], dhy.at[k], sp_send.at[3, k], sp_recv.at[3, k], (across, f)
+            dhp.at[part_of(zz, 1 - y), :], dhy.at[k], sp_out.at[DHY], sp_in.at[DHY_IN + k], (across, f)
         )
     for k in steps:
         zz = lax.rem(z + k, 4)
-        arrived(dhy.at[k], sp_recv.at[3, k])
+        arrived(dhy.at[k], sp_in.at[DHY_IN + k])
         both = dhp[part_of(zz, y), :] + dhy[k]
         if k == 0:
             dhr[z] = both
         else:
             dhy[k] = both
             send(
-                dhy.at[k], dhr.at[z], sp_send.at[3, 4 + k], sp_recv.at[3, 4 + k], (line_peer(k), f)
+                dhy.at[k], dhr.at[z], sp_out.at[DHL], sp_in.at[DHL], (line_peer(k), f)
             )
-    share_blocks(1, own_d1)
+    for n in range(4):
+        share_piece(1, n)
 
     first_tap = (s * R) // 512
 
@@ -883,11 +892,10 @@
             xt[t, p, i] = lifted(moved[0:1], moved[7:8] * ok)
         return carry
 
-    arrived(h1.at[f_x], f_recv.at[1, 0])
-    send(h1.at[f_x], h1.at[f_x], f_send.at[2, 0], f_recv.at[2, 0], (s, f_c))
+    arrived(h1.at[f_x], f_in.at[F_H1])
+    send(h1.at[f_x], h1.at[f_x], f_out.at[F_H1], f_in.at[F_H1C], (s, f_c))
     lax.fori_loop(0, 4 * F, tap_inputs, 0)
-    arrived(h1.at[f_c], f_recv.at[1, 1])
-    arrived(h1.at[f_d], f_recv.at[2, 0])
+    arrived(h1.at[0:2], f_in.at[F_H1C])
 
     def tap_hidden(n, carry):
         p, i = n // 4, lax.rem(n, 4)
@@ -915,11 +923,11 @@
 
     q1 = moved_pixels(1)
 
-    for k in range(1, 4):
-        arrived(dhr.at[lax.rem(z + 4 - k, 4)], sp_recv.at[3, 4 + k])
+    arrived(dhr.at[0:3], sp_in.at[DHL])
     d_hidden0 = (dhr[0] + dhr[1]) + (dhr[2] + dhr[3])
     unused, d_head0, d_gain0, d_shift0 = cell_backward(0, d_hidden0, d_cell0, None)
-    own_d0 = share_gates(0)
+    share_gates(0)
+    share_piece(0, 0)
 
     q = q1 + moved_pixels(0)
     total_w = jnp.zeros((128, 256), F32)
@@ -933,7 +941,8 @@
     lift_w = jnp.sum(total_w, axis=0, keepdims=True)
     lift_b = jnp.sum(total_b, axis=0, keepdims=True)
 
-    share_blocks(0, own_d0)
+    for n in range(1, 4):
+        share_piece(0, n)
 
     lane_sq = lax.broadcasted_iota(jnp.int32, (128, 128), 1)
     d_head = jnp.concatenate(
@@ -948,17 +957,20 @@
          jnp.zeros((1, 128), F32)], axis=0,
     )
     vf[f] = vt[...]
-    for n, p in enumerate(fpeers):
-        send(vt, vf.at[f], f_send.at[5, n], f_recv.at[5, n], (s, p))
-    relay_blocks(1)
-    for n, p in enumerate(fpeers):
-        arrived(vf.at[p], f_recv.at[5, n])
+    for p in fpeers:
+        send(vt, vf.at[f], f_out.at[F_VEC], f_in.at[F_VEC], (s, p))
+    for n in range(4):
+        relay_piece(1, n)
+    arrived(vf.at[0:3], f_in.at[F_VEC])
     vs[s] = (vf[0] + vf[1]) + (vf[2] + vf[3])
-    for k in range(1, S):
-        send(vs.at[s], vs.at[s], sp_send.at[7, k], sp_recv.at[7, k], (ahead(k), f))
-
-    relay_blocks(0)
-    gathered(1)
+    each(1, S, lambda k: send(
+        vs.at[s], vs.at[s], sp_out.at[VEC], sp_in.at[VEC], (ahead(k), f)
+    ))
+
+    for n in range(4):
+        relay_piece(0, n)
+    for n in range(4):
+        gathered(1, n)
 
     def grad_one(i, carry):
         for kind in range(2):
@@ -971,15 +983,13 @@
 
     lax.fori_loop(0, 4, grad_one, 0)
 
-    for k in range(1, S):
-        arrived(hr.at[behind(k)], sp_recv.at[6, k])
+    arrived(hr.at[1:S], sp_in.at[END])
     for k in range(S):
         for r in range(2):
             h_ref[16 * r : 16 * r + 16, 32 * k : 32 * k + 32] = hr[k, :, 64 * r : 64 * r + 32]
             c_ref[16 * r : 16 * r + 16, 32 * k : 32 * k + 32] = hr[k, :, 64 * r + 32 : 64 * r + 64]
 
-    for k in range(1, S):
-        arrived(vs.at[behind(k)], sp_recv.at[7, k])
+    arrived(vs.at[1:S], sp_in.at[VEC])
     lane8 = lax.broadcasted_iota(jnp.int32, (8, 128), 1)
     sub8 = lax.broadcasted_iota(jnp.int32, (8, 128), 0)
     lift = vs[0]
@@ -1011,18 +1021,14 @@
     for k in range(HOR):
         loss = loss + vs[s][2:3, 32 + k : 33 + k] * weight_rows[k]
 
-    gathered(0)
-
-    def grad_zero(i, carry):
-        total = None
-        for p in range(F):
-            part = dot(xt[0, p, i], dt[p])
-            total = part if total is None else total + part
-        at = pl.ds(pl.multiple_of(512 * i, 256), 256)
-        grad[at, :] = grad[at, :] + total
-        return carry
-
-    lax.fori_loop(0, 4, grad_zero, 0)
+    for n in range(4):
+        p = gathered(0, n)
+
+        def grad_zero(i):
+            at = pl.ds(pl.multiple_of(512 * i, 256), 256)
+            grad[at, :] = grad[at, :] + dot(xt[0, p, i], dt[p])
+
+        each(0, 4, grad_zero)
 
     def square(n, carry):
         v = grad[pl.ds(pl.multiple_of(base + 64 * n, 64), 64), :]
@@ -1030,15 +1036,14 @@
 
     total = lax.fori_loop(0, R // 64, square, jnp.zeros((64, 256), F32))
     qf[f] = jnp.full((8, 128), jnp.sum(total), F32)
-    for n, p in enumerate(fpeers):
-        send(qf.at[f], qf.at[f], f_send.at[6, n], f_recv.at[6, n], (s, p))
-    for n, p in enumerate(fpeers):
-        arrived(qf.at[p], f_recv.at[6, n])
+    for p in fpeers:
+        send(qf.at[f], qf.at[f], f_out.at[F_SQ], f_in.at[F_SQ], (s, p))
+    arrived(qf.at[0:3], f_in.at[F_SQ])
     qs[s] = (qf[0] + qf[1]) + (qf[2] + qf[3])
-    for k in range(1, S):
-        send(qs.at[s], qs.at[s], sp_send.at[8, k], sp_recv.at[8, k], (ahead(k), f))
-    for k in range(1, S):
-        arrived(qs.at[behind(k)], sp_recv.at[8, k])
+    each(1, S, lambda k: send(
+        qs.at[s], qs.at[s], sp_out.at[SQ], sp_in.at[SQ], (ahead(k), f)
+    ))
+    arrived(qs.at[1:S], sp_in.at[SQ])
     squares = qs[0]
     for k in range(1, S):
         squares = squares + qs[k]
@@ -1052,8 +1057,28 @@
 
     for cp in moments:
         cp.wait()
-    for cp, when in pending:
-        only(when, cp.wait_send)
+    for kind in range(2):
+        blocks = sum(len(holders(kind, i)) for i in range(4)) // 4
+        for i in range(4):
+            sent = functools.partial(left, wr.at[1:S, kind, i, :, f], w_out.at[kind, i])
+            only(holds(s, kind, i), sent)
+        for hop in range(3):
+            left(wr.at[0:blocks, kind, :, :, f], x_out.at[kind, hop])
+    left(tiles.at[f, 1:S], sp_out.at[TILE])
+    left(h1.at[f, 32 : 32 * S, :], sp_out.at[H1])
+    left(yrow.at[1:S], sp_out.at[Y])
+    left(dhy, sp_out.at[DHY])
+    left(dhr.at[0:3], sp_out.at[DHL])
+    for t in range(2):
+        left(dall.at[t, :, 1:S], sp_out.at[BLK + t])
+        left(dall.at[t, 0:3, s], f_out.at[F_D + t])
+    left(hr.at[1:S], sp_out.at[END])
+    left(vs.at[1:S], sp_out.at[VEC])
+    left(qs.at[1:S], sp_out.at[SQ])
+    left(tiles.at[0:3], f_out.at[F_TILE])
+    left(h1.at[0:3], f_out.at[F_H1])
+    left(vf.at[0:3], f_out.at[F_VEC])
+    left(qf.at[0:3], f_out.at[F_SQ])
 
 
 def sse_rows(sse):
@@ -1105,7 +1130,7 @@
             VM((128, PX), F32),
             VM((2, 3, 128, PX), F32),
             VM((F, 256, PX), BF16),
-            VM((S, 8, PX), F32),
+            VM((S, 2, PX), F32),
             VM((640, PX), BF16),
             VM((256, PX), F32),
             VM((4, 32, PX), F32),
@@ -1124,15 +1149,15 @@
             VM((S, 8, 128), F32),
             DMA((8,)),
             DMA((4,)),
-            DMA((6,)),
-            DMA((9, S)),
-            DMA((9, S)),
-            DMA((2, 4, S)),
-            DMA((2, 4, S)),
-            DMA((2, 4, S, 3)),
-            DMA((2, 4, S, 3)),
-            DMA((7, 3)),
-            DMA((7, 3)),
+            DMA((2, 4)),
+            DMA((2, 4)),
+            DMA((2, 3)),
+            DMA((2, 4)),
+            DMA((2, 2)),
+            DMA((10,)),
+            DMA((30,)),
+            DMA((7,)),
+            DMA((11,)),
         ],
         compiler_params=pltpu.CompilerParams(
             collective_id=0, has_side_effects=True, vmem_limit_bytes=44 * 2**20
@@ -1149,63 +1174,63 @@
     return out
 
 
-def adam_kernel(
-    steps,
-    small_ref, h_ref, c_ref, g_ref,
-    w_ref, m_ref, v_ref, gw_ref, gm_ref, gv_ref, cw_ref, cm_ref, cv_ref,
-    loss_ref, norm_ref,
-    wo_ref, mo_ref, vo_ref, gwo_ref, gmo_ref, gvo_ref, cwo_ref, cmo_ref, cvo_ref,
-    ho_ref, co_ref,
-    held, sems,
-):
+def adam_kernel(steps, *refs):
+    small_ref, h_ref, c_ref, g_ref = refs[:4]
+    (w_ref, m_ref, v_ref), gates, chan = refs[4:7], refs[7:10], refs[10:13]
+    outs, held, sem, sems = refs[13:26], refs[26:39], refs[39], refs[40]
+    conv_held, conv_outs = held[2:5], outs[2:5]
     factor = small_ref[5:6, 0:1]
     R = m_ref.shape[0]
     size = R // steps
     base = lax.rem(lax.axis_index("space") * R, 512)
+    held[0][...] = small_ref[3:4, 0:1]
+    held[1][...] = small_ref[4:5, 0:1]
+
+    def update(weights, grad, news):
+        w, m, v = weights
+        for ref, new in zip(news, adam_update(w[...], m[...], v[...], grad * factor)):
+            ref[...] = new
+
+    update(gates, small_ref[0:2, :], held[5:8])
+    chans = [small_ref[2:3, 32 * q : 32 * q + 32] for q in range(3)]
+    update(chan, jnp.concatenate(chans, axis=0), held[8:11])
+    for r in range(2):
+        held[11][0, r] = h_ref[16 * r : 16 * r + 16, :]
+        held[12][0, r] = c_ref[16 * r : 16 * r + 16, :]
     copies = []
+    for n in (0, 1, *range(5, 13)):
+        copies.append(pltpu.make_async_copy(held[n], outs[n], sem.at[n]))
+        copies[-1].start()
     for n in range(steps):
         at = slice(size * n, size * n + size)
         moved = pl.ds(pl.multiple_of(base + size * n, 64), size)
         news = adam_update(w_ref[moved, :], m_ref[at, :], v_ref[at, :], g_ref[moved, :] * factor)
-        for q, (new, out) in enumerate(zip(news, (wo_ref, mo_ref, vo_ref))):
-            held[q, at, :] = new
-            copy = pltpu.make_async_copy(held.at[q, at, :], out.at[at, :], sems.at[q, n])
-            copy.start()
-            copies.append(copy)
-
-    def update(w, m, v, grad, outs):
-        for ref, new in zip(outs, adam_update(w[...], m[...], v[...], grad * factor)):
-            ref[...] = new
-
-    loss_ref[...] = small_ref[3:4, 0:1]
-    norm_ref[...] = small_ref[4:5, 0:1]
-    update(gw_ref, gm_ref, gv_ref, small_ref[0:2, :], (gwo_ref, gmo_ref, gvo_ref))
-    chans = [small_ref[2:3, 32 * q : 32 * q + 32] for q in range(3)]
-    update(cw_ref, cm_ref, cv_ref, jnp.concatenate(chans, axis=0), (cwo_ref, cmo_ref, cvo_ref))
-    for r in range(2):
-        ho_ref[0, r] = h_ref[16 * r : 16 * r + 16, :]
-        co_ref[0, r] = c_ref[16 * r : 16 * r + 16, :]
+        for q, new in enumerate(news):
+            conv_held[q][at, :] = new
+            copies.append(
+                pltpu.make_async_copy(conv_held[q].at[at, :], conv_outs[q].at[at, :], sems.at[q, n])
+            )
+            copies[-1].start()
     for copy in copies:
         copy.wait()
 
 
 def adam_step(small, hidden, cell, grad, weights, frame_shape):
-    R, N = weights[0][1].shape
     steps = 5
     rows, cols = frame_shape
-    vmem, any_ = pl.BlockSpec(memory_space=pltpu.VMEM), pl.BlockSpec(memory_space=pl.ANY)
     conv, gates, chan = weights
     flat = [*conv, *gates, *chan]
-    shapes = [jax.ShapeDtypeStruct(v.shape, F32) for v in (*conv[1:], conv[1], *gates, *chan)]
-    scalar = jax.ShapeDtypeStruct((1, 1), F32)
-    state = jax.ShapeDtypeStruct((1, rows, cols, hidden.shape[1]), F32)
+    shapes = [v.shape for v in (*conv[1:], conv[1], *gates, *chan)]
+    state = (1, rows, cols, hidden.shape[1])
+    shapes = [(1, 1), (1, 1), *shapes, state, state]
     out = pl.pallas_call(
         functools.partial(adam_kernel, steps),
-        out_shape=(scalar, scalar, *shapes, state, state),
-        in_specs=[vmem] * (4 + len(flat)),
-        out_specs=(vmem, vmem, *([any_] * 3), *([vmem] * 8)),
-        scratch_shapes=[pltpu.VMEM((3, R, N), F32), pltpu.SemaphoreType.DMA((3, steps))],
-        compiler_params=pltpu.CompilerParams(vmem_limit_bytes=7 * 2**20),
+        out_shape=tuple(jax.ShapeDtypeStruct(v, F32) for v in shapes),
+        in_specs=[pl.BlockSpec(memory_space=pltpu.VMEM)] * (4 + len(flat)),
+        out_specs=(pl.BlockSpec(memory_space=pl.ANY),) * len(shapes),
+        scratch_shapes=[pltpu.VMEM(v, F32) for v in shapes]
+        + [pltpu.SemaphoreType.DMA((13,)), pltpu.SemaphoreType.DMA((3, steps))],
+        compiler_params=pltpu.CompilerParams(vmem_limit_bytes=8 * 2**20),
     )(small, hidden, cell, grad, *flat)
     return (out[0].reshape(()), out[1].reshape(()), *out[2:])
 

time: 117 us -> 106 us (0.906)
  Pallas kernels: 116 us -> 104 us
    pallas_call x1, Pallas kernels: 111 us -> 101 us  [step_fast(): pl.pallas_call(functools.partial(step_kernel, geo), out_shape=(VM((2048,...]
where the time goes in v2:
time: 106 us; the launch traced here: 105 us
  Pallas kernels  104 us (98%)
    pallas_call x1, Pallas kernels, step_fast(): pl.pallas_call(functools.partial(step_kernel, geo), out_shape=(VM((2048,...  101 us
    pallas_call x1, Pallas kernels, adam_step(): pl.pallas_call(functools.partial(adam_kernel, steps), out_shape=tuple((ja...  3.76 us

profile of v2, /device:TPU:0, one launch (start us, length us, event | category | flops | bytes accessed | tf_op | source)
XLA Modules:
  0.0 105.4 jit_solution(237161212424730095)
XLA Ops:
  0.6 0.0 copy-start
  0.7 0.0 copy-start.1
  0.7 0.0 copy-start.2
  0.7 0.0 copy-start.3
  0.7 0.0 copy-start.4
  0.7 0.0 copy-start.5
  0.7 100.7 %shard_map.228 = (f32[2048,256]{1,0:T(8,128)S(1)}, f32[2048,256]{1,0:T(8,128)S(1)}, f32[1600,256]{1,0:T(8,128)S(1)}, f32[1600,256]{1,0:T(8,128)S(1)}, f32[8,128]...) custom-call(f32[2,1,2,2,16]{4,3,2,1,0:T(2,128)} %frames_in.1, f32[2,1,2,2,16]{4,3,2,1,0:T(2,128)} %targets_in.1, ...), custom_call_target="tpu_custom_call" | custom-call | tf_op jit(solution)/shard_map/pallas_call | solution.py:1099
  101.4 0.0 copy-done
  101.4 0.0 copy-done.1
  101.4 0.0 copy-done.2
  101.4 0.0 copy-done.3
  101.4 0.0 copy-done.4
  101.4 0.0 copy-done.5
  101.4 3.8 %shard_map.229 = (f32[1,1]{1,0:T(1,128)}, f32[1,1]{1,0:T(1,128)}, f32[1600,256]{1,0:T(8,128)}, f32[1600,256]{1,0:T(8,128)}, f32[1600,256]{1,0:T(8,128)}, /*index...) custom-call(f32[8,128]{1,0:T(8,128)S(1)} %get-tuple-element.33.refs_, ...), custom_call_target="tpu_custom_call" | custom-call | tf_op jit(solution)/shard_map/pallas_call | solution.py:1226
Async XLA Ops:
  0.6 100.7 %copy-start = (f32[3,32]{1,0:T(4,128)S(1)}, f32[3,32]{1,0:T(4,128)}, u32[]{:S(2)}) copy-start(f32[3,32]{1,0:T(4,128)} %refs_10_.1) | copy-start | bytes 1156
  0.7 100.7 %copy-start.1 = (f32[2,128]{1,0:T(2,128)S(1)}, f32[2,128]{1,0:T(2,128)}, u32[]{:S(2)}) copy-start(f32[2,128]{1,0:T(2,128)} %refs_7_.1) | copy-start | bytes 3076
  0.7 100.7 %copy-start.2 = (f32[3,32]{1,0:T(4,128)S(1)}, f32[3,32]{1,0:T(4,128)}, u32[]{:S(2)}) copy-start(f32[3,32]{1,0:T(4,128)} %refs_11_.1) | copy-start | bytes 1156
  0.7 100.7 %copy-start.3 = (f32[3,32]{1,0:T(4,128)S(1)}, f32[3,32]{1,0:T(4,128)}, u32[]{:S(2)}) copy-start(f32[3,32]{1,0:T(4,128)} %refs_12_.1) | copy-start | bytes 1156
  0.7 100.7 %copy-start.4 = (f32[2,128]{1,0:T(2,128)S(1)}, f32[2,128]{1,0:T(2,128)}, u32[]{:S(2)}) copy-start(f32[2,128]{1,0:T(2,128)} %refs_8_.1) | copy-start | bytes 3076
  0.7 100.7 %copy-start.5 = (f32[2,128]{1,0:T(2,128)S(1)}, f32[2,128]{1,0:T(2,128)}, u32[]{:S(2)}) copy-start(f32[2,128]{1,0:T(2,128)} %refs_9_.1) | copy-start | bytes 3076

commit v3 on v2

--- a/solution.py
+++ b/solution.py
@@ -360,6 +360,8 @@
     c_in,
     sp_out,
     sp_in,
+    y_out,
+    chain_in,
     f_out,
     f_in,
 ):
@@ -494,8 +496,9 @@
     for i in order[0][1:]:
         stage_slot(0, i)
         send_slot(0, i)
-    stage_slot(1, order[1][0])
-    stage_slot(1, order[1][1])
+    for i in order[1]:
+        stage_slot(1, i)
+        send_slot(1, i)
     for i in range(4):
         wr[s, 0, i, :, f] = stage[0, i, :, s]
 
@@ -589,18 +592,21 @@
 
             each(0, S, hop)
 
-        for n, i in enumerate(order[kind]):
-            first_hop(i)
-            if kind == 0 and n > 0:
-                send_slot(1, order[1][n - 1])
-            if kind == 0 and n == 3:
-                send_slot(1, order[1][3])
-            if n > 0:
-                second_hop(order[kind][n - 1])
-        second_hop(order[kind][3])
-        blocks = sum(counts) // 4
-        arrived(wr.at[0:blocks, kind, :, :, f_c], c_in.at[kind, 0])
-        arrived(wr.at[0:blocks, kind, :, :, f_d], c_in.at[kind, 1])
+        def finish():
+            blocks = sum(counts) // 4
+            arrived(wr.at[0:blocks, kind, :, :, f_c], c_in.at[kind, 0])
+            arrived(wr.at[0:blocks, kind, :, :, f_d], c_in.at[kind, 1])
+
+        def first(n):
+            first_hop(order[kind][n])
+
+        def second(n):
+            second_hop(order[kind][n])
+
+        return first, second, finish
+
+    first_l, second_l, finish_l = relay(0)
+    first_h, second_h, finish_h = relay(1)
 
     def merge(kind, out):
         for tap in range(TAPS):
@@ -683,12 +689,17 @@
     ]
     for cp in moments:
         cp.start()
-    stage_slot(1, order[1][2])
-    stage_slot(1, order[1][3])
+    slid_lift(0)
     for i in range(4):
         wr[s, 1, i, :, f] = stage[1, i, :, s]
-    slid_lift(0)
-    relay(0)
+    first_l(0)
+    for n in range(1, 4):
+        first_l(n)
+        second_l(n - 1)
+    first_h(0)
+    second_l(3)
+    first_h(1)
+    finish_l()
     merge(0, wl)
     hidden0, cell0 = cell_forward(0, conv(wl), None)
     mine = pl.ds(pl.multiple_of(32 * s, 32), 32)
@@ -697,7 +708,13 @@
         h1.at[f, mine, :], h1.at[f, mine, :], sp_out.at[H1], sp_in.at[H1], (ahead(k), f)
     ))
 
-    relay(1)
+    first_h(2)
+    second_h(0)
+    second_h(1)
+    first_h(3)
+    second_h(2)
+    second_h(3)
+    finish_h()
     slid_lift(1)
     pre1[...] = conv(wl)
     merge(1, wh)
@@ -821,18 +838,51 @@
         block = dall.at[t, p, s]
         if peer is not None:
             arrived(block, f_in.at[F_D + 3 * t + peer])
-        for k in (2, 3, 1):
-            send(
-                block, block, sp_out.at[BLK + t], sp_in.at[LINE_IN + 4 * t + n], (line_peer(k), f)
-            )
-        send(block, block, sp_out.at[BLK + t], sp_in.at[ACROSS_IN + 4 * t + n], (across, f))
-
-    def relay_piece(t, n):
+        if CHAIN[t]:
+            for way in range(2):
+                pass_on(t, n, 0, way, block)
+        else:
+            for k in (2, 3, 1):
+                send(
+                    block, block, sp_out.at[BLK + t], sp_in.at[LINE_IN + 4 * t + n],
+                    (line_peer(k), f),
+                )
+        send(block, block, y_out.at[t], sp_in.at[ACROSS_IN + 4 * t + n], (across, f))
+
+    def pass_on(t, n, hop, way, block):
+        inside_line, to = ((z < 3, z + 1), (z > 0, z - 1))[way]
+        pl.when(inside_line)(lambda: send(
+            block, block, sp_out.at[BLK + t], chain_in.at[t, n, hop, way], (2 * to + y, f)
+        ))
+
+    def relay_hop(t, n, hop):
+        p, unused = pieces[n]
+        for way, there in ((0, z >= hop), (1, z + hop <= 3)):
+            block = dall.at[t, p, 2 * lax.rem(z + (4 - hop, hop)[way], 4) + y]
+
+            def come():
+                arrived(block, chain_in.at[t, n, hop - 1, way])
+                if hop < 3:
+                    pass_on(t, n, hop, way, block)
+                send(block, block, y_out.at[t], sp_in.at[ACROSS_IN + 4 * t + n], (across, f))
+
+            pl.when(there)(come)
+
+    def relay_wave(t, wave):
+        if CHAIN[t]:
+            for hop in range(1, 4):
+                if 0 <= wave - hop < 4:
+                    relay_hop(t, wave - hop, hop)
+            return
+        n = wave - 1
         p, unused = pieces[n]
         arrived(dall.at[t, p, 0:3], sp_in.at[LINE_IN + 4 * t + n])
         for k in (1, 3, 2):
             block = dall.at[t, p, line_source(k)]
-            send(block, block, sp_out.at[BLK + t], sp_in.at[ACROSS_IN + 4 * t + n], (across, f))
+            send(block, block, y_out.at[t], sp_in.at[ACROSS_IN + 4 * t + n], (across, f))
+
+    CHAIN = (True, False)
+    WAVES = [6 if chain else 4 for chain in CHAIN]
 
     def gathered(t, n):
         p, unused = pieces[n]
@@ -941,8 +991,12 @@
     lift_w = jnp.sum(total_w, axis=0, keepdims=True)
     lift_b = jnp.sum(total_b, axis=0, keepdims=True)
 
-    for n in range(1, 4):
+    relay_wave(1, 1)
+    share_piece(0, 1)
+    relay_wave(1, 2)
+    for n in range(2, 4):
         share_piece(0, n)
+    relay_wave(1, 3)
 
     lane_sq = lax.broadcasted_iota(jnp.int32, (128, 128), 1)
     d_head = jnp.concatenate(
@@ -959,16 +1013,16 @@
     vf[f] = vt[...]
     for p in fpeers:
         send(vt, vf.at[f], f_out.at[F_VEC], f_in.at[F_VEC], (s, p))
-    for n in range(4):
-        relay_piece(1, n)
+    for wave in range(4, WAVES[1] + 1):
+        relay_wave(1, wave)
     arrived(vf.at[0:3], f_in.at[F_VEC])
     vs[s] = (vf[0] + vf[1]) + (vf[2] + vf[3])
     each(1, S, lambda k: send(
         vs.at[s], vs.at[s], sp_out.at[VEC], sp_in.at[VEC], (ahead(k), f)
     ))
 
-    for n in range(4):
-        relay_piece(0, n)
+    for wave in range(1, WAVES[0] + 1):
+        relay_wave(0, wave)
     for n in range(4):
         gathered(1, n)
 
@@ -1070,7 +1124,14 @@
     left(dhy, sp_out.at[DHY])
     left(dhr.at[0:3], sp_out.at[DHL])
     for t in range(2):
-        left(dall.at[t, :, 1:S], sp_out.at[BLK + t])
+        left(dall.at[t, :, 0:4], y_out.at[t])
+        if CHAIN[t]:
+            edge = (z == 0) | (z == 3)
+            pl.when(edge)(lambda: left(dall.at[t, :, 0:1], sp_out.at[BLK + t]))
+            middle = jnp.logical_not(edge)
+            pl.when(middle)(lambda: left(dall.at[t, :, 0:5], sp_out.at[BLK + t]))
+        else:
+            left(dall.at[t, :, 0:3], sp_out.at[BLK + t])
         left(dall.at[t, 0:3, s], f_out.at[F_D + t])
     left(hr.at[1:S], sp_out.at[END])
     left(vs.at[1:S], sp_out.at[VEC])
@@ -1156,6 +1217,8 @@
             DMA((2, 2)),
             DMA((10,)),
             DMA((30,)),
+            DMA((2,)),
+            DMA((2, 4, 3, 2)),
             DMA((7,)),
             DMA((11,)),
         ],

time: 106 us -> 102 us (0.962)
  Pallas kernels: 104 us -> 101 us
    pallas_call x1, Pallas kernels: 101 us -> 96.8 us  [step_fast(): pl.pallas_call(functools.partial(step_kernel, geo), out_shape=(VM((2048,...]
where the time goes in v3:
time: 102 us
  Pallas kernels  101 us (99%)
    pallas_call x1, Pallas kernels, step_fast(): pl.pallas_call(functools.partial(step_kernel, geo), out_shape=(VM((2048,...  96.8 us
    pallas_call x1, Pallas kernels, adam_step(): pl.pallas_call(functools.partial(adam_kernel, steps), out_shape=tuple((ja...  3.76 us

profile of v3, /device:TPU:0, one launch (start us, length us, event | category | flops | bytes accessed | tf_op | source)
XLA Modules:
  0.0 101.5 jit_solution(8090693420399564996)
XLA Ops:
  0.6 0.0 copy-start
  0.7 0.0 copy-start.1
  0.7 0.0 copy-start.2
  0.7 0.0 copy-start.3
  0.7 0.0 copy-start.4
  0.7 0.0 copy-start.5
  0.7 96.8 %shard_map.228 = (f32[2048,256]{1,0:T(8,128)S(1)}, f32[2048,256]{1,0:T(8,128)S(1)}, f32[1600,256]{1,0:T(8,128)S(1)}, f32[1600,256]{1,0:T(8,128)S(1)}, f32[8,128]...) custom-call(f32[2,1,2,2,16]{4,3,2,1,0:T(2,128)} %frames_in.1, f32[2,1,2,2,16]{4,3,2,1,0:T(2,128)} %targets_in.1, ...), custom_call_target="tpu_custom_call" | custom-call | tf_op jit(solution)/shard_map/pallas_call | solution.py:1160
  97.5 0.0 copy-done
  97.5 0.0 copy-done.1
  97.6 0.0 copy-done.2
  97.6 0.0 copy-done.3
  97.6 0.0 copy-done.4
  97.6 0.0 copy-done.5
  97.6 3.8 %shard_map.229 = (f32[1,1]{1,0:T(1,128)}, f32[1,1]{1,0:T(1,128)}, f32[1600,256]{1,0:T(8,128)}, f32[1600,256]{1,0:T(8,128)}, f32[1600,256]{1,0:T(8,128)}, /*index...) custom-call(f32[8,128]{1,0:T(8,128)S(1)} %get-tuple-element.33.refs_, ...), custom_call_target="tpu_custom_call" | custom-call | tf_op jit(solution)/shard_map/pallas_call | solution.py:1289
Async XLA Ops:
  0.6 96.9 %copy-start = (f32[3,32]{1,0:T(4,128)S(1)}, f32[3,32]{1,0:T(4,128)}, u32[]{:S(2)}) copy-start(f32[3,32]{1,0:T(4,128)} %refs_10_.1) | copy-start | bytes 1156
  0.7 96.9 %copy-start.1 = (f32[2,128]{1,0:T(2,128)S(1)}, f32[2,128]{1,0:T(2,128)}, u32[]{:S(2)}) copy-start(f32[2,128]{1,0:T(2,128)} %refs_7_.1) | copy-start | bytes 3076
  0.7 96.9 %copy-start.2 = (f32[3,32]{1,0:T(4,128)S(1)}, f32[3,32]{1,0:T(4,128)}, u32[]{:S(2)}) copy-start(f32[3,32]{1,0:T(4,128)} %refs_11_.1) | copy-start | bytes 1156
  0.7 96.9 %copy-start.3 = (f32[3,32]{1,0:T(4,128)S(1)}, f32[3,32]{1,0:T(4,128)}, u32[]{:S(2)}) copy-start(f32[3,32]{1,0:T(4,128)} %refs_12_.1) | copy-start | bytes 1156
  0.7 96.9 %copy-start.4 = (f32[2,128]{1,0:T(2,128)S(1)}, f32[2,128]{1,0:T(2,128)}, u32[]{:S(2)}) copy-start(f32[2,128]{1,0:T(2,128)} %refs_8_.1) | copy-start | bytes 3076
  0.7 96.9 %copy-start.5 = (f32[2,128]{1,0:T(2,128)S(1)}, f32[2,128]{1,0:T(2,128)}, u32[]{:S(2)}) copy-start(f32[2,128]{1,0:T(2,128)} %refs_9_.1) | copy-start | bytes 3076

commit v4 on v3

--- a/solution.py
+++ b/solution.py
@@ -754,6 +754,21 @@
     )
     hr[s] = ht[s]
 
+    first_tap = (s * R) // 512
+
+    def tap_inputs(n, carry):
+        p, i = n // 4, lax.rem(n, 4)
+        tap = first_tap + i
+        da, db = tap // 5 - 2, lax.rem(tap, 5) - 2
+        back = lax.rem(2 * PX - 32 * da - db, PX)
+        ok = (row_of + da >= 0) & (row_of + da < rows) & (col_of + db >= 0) & (col_of + db < 16)
+        ok = ok.astype(F32)
+        for t in range(2):
+            moved = pltpu.roll(pix[p, t], back, 1)
+            xt[t, p, i] = lifted(moved[0:1], moved[7:8] * ok)
+        return carry
+
+    lax.fori_loop(0, 4 * F, tap_inputs, 0)
     arrived(yrow.at[1:S], sp_in.at[Y])
     ysum = yrow[0]
     for k in range(1, S):
@@ -928,23 +943,8 @@
     for n in range(4):
         share_piece(1, n)
 
-    first_tap = (s * R) // 512
-
-    def tap_inputs(n, carry):
-        p, i = n // 4, lax.rem(n, 4)
-        tap = first_tap + i
-        da, db = tap // 5 - 2, lax.rem(tap, 5) - 2
-        back = lax.rem(2 * PX - 32 * da - db, PX)
-        ok = (row_of + da >= 0) & (row_of + da < rows) & (col_of + db >= 0) & (col_of + db < 16)
-        ok = ok.astype(F32)
-        for t in range(2):
-            moved = pltpu.roll(pix[p, t], back, 1)
-            xt[t, p, i] = lifted(moved[0:1], moved[7:8] * ok)
-        return carry
-
     arrived(h1.at[f_x], f_in.at[F_H1])
     send(h1.at[f_x], h1.at[f_x], f_out.at[F_H1], f_in.at[F_H1C], (s, f_c))
-    lax.fori_loop(0, 4 * F, tap_inputs, 0)
     arrived(h1.at[0:2], f_in.at[F_H1C])
 
     def tap_hidden(n, carry):
@@ -1037,6 +1037,23 @@
 
     lax.fori_loop(0, 4, grad_one, 0)
 
+    for n in range(4):
+        p = gathered(0, n)
+
+        def grad_zero(i):
+            at = pl.ds(pl.multiple_of(512 * i, 256), 256)
+            grad[at, :] = grad[at, :] + dot(xt[0, p, i], dt[p])
+
+        each(0, 4, grad_zero)
+
+    def square(n, carry):
+        v = grad[pl.ds(pl.multiple_of(base + 64 * n, 64), 64), :]
+        return carry + v * v
+
+    total = lax.fori_loop(0, R // 64, square, jnp.zeros((64, 256), F32))
+    qf[f] = jnp.full((8, 128), jnp.sum(total), F32)
+    for p in fpeers:
+        send(qf.at[f], qf.at[f], f_out.at[F_SQ], f_in.at[F_SQ], (s, p))
     arrived(hr.at[1:S], sp_in.at[END])
     for k in range(S):
         for r in range(2):
@@ -1075,23 +1092,6 @@
     for k in range(HOR):
         loss = loss + vs[s][2:3, 32 + k : 33 + k] * weight_rows[k]
 
-    for n in range(4):
-        p = gathered(0, n)
-
-        def grad_zero(i):
-            at = pl.ds(pl.multiple_of(512 * i, 256), 256)
-            grad[at, :] = grad[at, :] + dot(xt[0, p, i], dt[p])
-
-        each(0, 4, grad_zero)
-
-    def square(n, carry):
-        v = grad[pl.ds(pl.multiple_of(base + 64 * n, 64), 64), :]
-        return carry + v * v
-
-    total = lax.fori_loop(0, R // 64, square, jnp.zeros((64, 256), F32))
-    qf[f] = jnp.full((8, 128), jnp.sum(total), F32)
-    for p in fpeers:
-        send(qf.at[f], qf.at[f], f_out.at[F_SQ], f_in.at[F_SQ], (s, p))
     arrived(qf.at[0:3], f_in.at[F_SQ])
     qs[s] = (qf[0] + qf[1]) + (qf[2] + qf[3])
     each(1, S, lambda k: send(
@@ -1279,7 +1279,7 @@
 
 
 def adam_step(small, hidden, cell, grad, weights, frame_shape):
-    steps = 5
+    steps = 25
     rows, cols = frame_shape
     conv, gates, chan = weights
     flat = [*conv, *gates, *chan]

time: 102 us -> 101 us (level)
  no operation moved by 1% of the time
where the time goes in v4:
time: 101 us
  Pallas kernels  100 us (99%)
    pallas_call x1, Pallas kernels, step_fast(): pl.pallas_call(functools.partial(step_kernel, geo), out_shape=(VM((2048,...  96.7 us
    pallas_call x1, Pallas kernels, adam_step(): pl.pallas_call(functools.partial(adam_kernel, steps), out_shape=tuple((ja...  3.24 us

profile of v4, /device:TPU:0, one launch (start us, length us, event | category | flops | bytes accessed | tf_op | source)
XLA Modules:
  0.0 100.9 jit_solution(7730267959564751620)
XLA Ops:
  0.6 0.0 copy-start
  0.7 0.0 copy-start.1
  0.7 0.0 copy-start.2
  0.7 0.0 copy-start.3
  0.7 0.0 copy-start.4
  0.7 0.0 copy-start.5
  0.7 96.7 %shard_map.228 = (f32[2048,256]{1,0:T(8,128)S(1)}, f32[2048,256]{1,0:T(8,128)S(1)}, f32[1600,256]{1,0:T(8,128)S(1)}, f32[1600,256]{1,0:T(8,128)S(1)}, f32[8,128]...) custom-call(f32[2,1,2,2,16]{4,3,2,1,0:T(2,128)} %frames_in.1, f32[2,1,2,2,16]{4,3,2,1,0:T(2,128)} %targets_in.1, ...), custom_call_target="tpu_custom_call" | custom-call | tf_op jit(solution)/shard_map/pallas_call | solution.py:1160
  97.5 0.0 copy-done
  97.5 0.0 copy-done.1
  97.5 0.0 copy-done.2
  97.5 0.0 copy-done.3
  97.5 0.0 copy-done.4
  97.5 0.0 copy-done.5
  97.5 3.2 %shard_map.229 = (f32[1,1]{1,0:T(1,128)}, f32[1,1]{1,0:T(1,128)}, f32[1600,256]{1,0:T(8,128)}, f32[1600,256]{1,0:T(8,128)}, f32[1600,256]{1,0:T(8,128)}, /*index...) custom-call(f32[8,128]{1,0:T(8,128)S(1)} %get-tuple-element.33.refs_, ...), custom_call_target="tpu_custom_call" | custom-call | tf_op jit(solution)/shard_map/pallas_call | solution.py:1289
Async XLA Ops:
  0.6 96.8 %copy-start = (f32[3,32]{1,0:T(4,128)S(1)}, f32[3,32]{1,0:T(4,128)}, u32[]{:S(2)}) copy-start(f32[3,32]{1,0:T(4,128)} %refs_10_.1) | copy-start | bytes 1156
  0.7 96.8 %copy-start.1 = (f32[2,128]{1,0:T(2,128)S(1)}, f32[2,128]{1,0:T(2,128)}, u32[]{:S(2)}) copy-start(f32[2,128]{1,0:T(2,128)} %refs_7_.1) | copy-start | bytes 3076
  0.7 96.8 %copy-start.2 = (f32[3,32]{1,0:T(4,128)S(1)}, f32[3,32]{1,0:T(4,128)}, u32[]{:S(2)}) copy-start(f32[3,32]{1,0:T(4,128)} %refs_11_.1) | copy-start | bytes 1156
  0.7 96.8 %copy-start.3 = (f32[3,32]{1,0:T(4,128)S(1)}, f32[3,32]{1,0:T(4,128)}, u32[]{:S(2)}) copy-start(f32[3,32]{1,0:T(4,128)} %refs_12_.1) | copy-start | bytes 1156
  0.7 96.8 %copy-start.4 = (f32[2,128]{1,0:T(2,128)S(1)}, f32[2,128]{1,0:T(2,128)}, u32[]{:S(2)}) copy-start(f32[2,128]{1,0:T(2,128)} %refs_8_.1) | copy-start | bytes 3076
  0.7 96.8 %copy-start.5 = (f32[2,128]{1,0:T(2,128)S(1)}, f32[2,128]{1,0:T(2,128)}, u32[]{:S(2)}) copy-start(f32[2,128]{1,0:T(2,128)} %refs_9_.1) | copy-start | bytes 3076
